TPU v7x, 128 devices: a whole 4x4x4 slice. The times are simulated.
128 devices in a mesh: section: 4 (over x), ctx: 32 (over z, y, core).
Axes of the slice: x: 4, y: 4, z: 4, core: 2. Of those that a mesh axis runs over, the one named last changes fastest.
Arguments:
- inputs: bfloat16 [2, 1, 2048, 1024], P(None, None, 'ctx'), may hold values from -6 to 6
- cotangent: bfloat16 [2, 1, 2048, 1024], P(None, None, 'ctx'), may hold values from -6 to 6
- segment_ids: int32 [2, 1, 2048], replicated, may hold values from 0 to 2, as said below
- gains: bfloat16 [4, 1024], P('section', 'ctx'), may hold values from 0.25 to 1.75
- wq1: bfloat16 [1024, 1024], P('ctx', 'section'), may hold values from -0.1875 to 0.1875
- wk1: bfloat16 [1024, 1024], P('ctx', 'section'), may hold values from -0.1875 to 0.1875
- wv1: bfloat16 [1024, 1024], P('ctx', 'section'), may hold values from -0.1875 to 0.1875
- wo1: bfloat16 [1024, 1024], P('ctx', 'section'), may hold values from -3 to 3
- wg1: bfloat16 [1024, 2816], P('ctx', 'section'), may hold values from -0.1875 to 0.1875
- wu1: bfloat16 [1024, 2816], P('ctx', 'section'), may hold values from -0.1875 to 0.1875
- wd1: bfloat16 [2816, 1024], P('ctx', 'section'), may hold values from -0.109375 to 0.109375
- wq2: bfloat16 [1024, 1024], P('ctx', 'section'), may hold values from -0.1875 to 0.1875
- wk2: bfloat16 [1024, 1024], P('ctx', 'section'), may hold values from -0.1875 to 0.1875
- wv2: bfloat16 [1024, 1024], P('ctx', 'section'), may hold values from -0.1875 to 0.1875
- wo2: bfloat16 [1024, 1024], P('ctx', 'section'), may hold values from -3 to 3
- wg2: bfloat16 [1024, 2816], P('ctx', 'section'), may hold values from -0.1875 to 0.1875
- wu2: bfloat16 [1024, 2816], P('ctx', 'section'), may hold values from -0.1875 to 0.1875
- wd2: bfloat16 [2816, 1024], P('ctx', 'section'), may hold values from -0.109375 to 0.109375
Outputs:
- outputs: bfloat16 [2, 1, 2048, 1024], P(None, None, 'ctx', 'section')
- input_grads: bfloat16 [2, 1, 2048, 1024], P(None, None, 'ctx', 'section')
- gain_grads: float32 [4, 1024], P('section', 'ctx')
- grad_wq1: float32 [1024, 1024], P('ctx', 'section')
- grad_wk1: float32 [1024, 1024], P('ctx', 'section')
- grad_wv1: float32 [1024, 1024], P('ctx', 'section')
- grad_wo1: float32 [1024, 1024], P('ctx', 'section')
- grad_wg1: float32 [1024, 2816], P('ctx', 'section')
- grad_wu1: float32 [1024, 2816], P('ctx', 'section')
- grad_wd1: float32 [2816, 1024], P('ctx', 'section')
- grad_wq2: float32 [1024, 1024], P('ctx', 'section')
- grad_wk2: float32 [1024, 1024], P('ctx', 'section')
- grad_wv2: float32 [1024, 1024], P('ctx', 'section')
- grad_wo2: float32 [1024, 1024], P('ctx', 'section')
- grad_wg2: float32 [1024, 2816], P('ctx', 'section')
- grad_wu2: float32 [1024, 2816], P('ctx', 'section')
- grad_wd2: float32 [2816, 1024], P('ctx', 'section')
Inputs may be any that keep to these rules, and one draw needn't show every extreme that they name: `segment_ids`: along each sequence the ids never fall, and each sequence holds each of the values 0, 1 and 2.
All inputs are finite; a program needn't handle non-finite values.
Results may differ from a plain program's by a relative error of at most 0.028.
Values may be sent and summed in bfloat16 or wider, within the bound.
A program may use at most 256 MiB of HBM per device.

v0:
```python
from types import SimpleNamespace

import jax
import jax.numpy as jnp
from jax import lax
from jax.experimental import pallas as pl
from jax.experimental.pallas import tpu as pltpu
from jax.sharding import PartitionSpec as P

MESH = pl.DeviceIdType.MESH
BF = jnp.bfloat16
F32 = jnp.float32
I32 = jnp.int32
EPS = 1e-06
MASKED = -1e30


def spec(dtype, *shape):
    return shape, dtype


LAYER_IN = dict(
    wq=spec(BF, 32, 256),
    wk=spec(BF, 32, 256),
    wv=spec(BF, 32, 256),
    wo=spec(BF, 32, 256),
    gus=spec(BF, 2, 32, 768),
    wd=spec(BF, 88, 256),
)
COMMON_IN = dict(
    xin=spec(BF, 2, 2, 32, 1024), cot=spec(BF, 2, 2, 32, 1024), gst=spec(F32, 8, 128), startq=spec(I32, 8, 512)
)
LAYER_OUT = dict(
    oq=spec(F32, 32, 256),
    ok=spec(F32, 32, 256),
    ov=spec(F32, 32, 256),
    oo=spec(F32, 32, 256),
    ogu=spec(F32, 2, 32, 768),
    od=spec(F32, 96, 256),
)
COMMON_OUT = dict(out=spec(BF, 2, 2, 32, 256), ing=spec(BF, 2, 2, 32, 256), ogg=spec(F32, 8, 128))
COMMON = dict(
    hin=spec(BF, 8, 32, 1024),
    gx=spec(F32, 3, 8, 128),
    g1=spec(F32, 8, 128),
    gyr=spec(F32, 8, 8, 128),
    gz=spec(F32, 4, 2, 8, 128),
    gains=spec(F32, 8, 1024),
    gg=spec(F32, 8, 1024),
    ggx=spec(F32, 3, 8, 1024),
    ggz=spec(F32, 4, 8, 256),
    ggzr=spec(F32, 3, 8, 256),
    ggy=spec(F32, 2, 8, 128),
    ggyr=spec(F32, 8, 8, 128),
    scores=spec(F32, 16, 128, 512),
    dkvf=spec(F32, 2, 256, 256),
    outst=spec(BF, 4, 32, 256),
    ingst=spec(BF, 4, 32, 256),
    outrv=spec(BF, 2, 2, 32, 256),
    ingrv=spec(BF, 2, 2, 32, 256),
    dmh=spec(BF, 256, 128),
)
LAYER = dict(
    wst=spec(BF, 2, 32, 384),
    wds=spec(BF, 96, 256),
    wqkv=spec(BF, 4, 8, 32, 384),
    wout=spec(BF, 4, 4, 32, 256),
    wgu=spec(BF, 4, 4, 2, 32, 768),
    wdn=spec(BF, 4, 4, 96, 256),
    kv=spec(BF, 4, 2, 256, 256),
    q2=spec(BF, 512, 128),
    prob=spec(BF, 16, 128, 512),
    ot=spec(F32, 128, 256),
    gu=spec(F32, 256, 768),
    hid=spec(BF, 256, 384),
    dkv=spec(BF, 4, 2, 256, 256),
    dkvr=spec(BF, 3, 2, 256, 256),
    dkvs=spec(BF, 256, 256),
    dkvy=spec(BF, 256, 256),
    gwqkv=spec(BF, 4, 8, 32, 384),
    gwout=spec(BF, 4, 4, 32, 256),
    gwgu=spec(BF, 4, 4, 2, 32, 768),
    gwdn=spec(BF, 4, 4, 96, 256),
    rzqkv=spec(BF, 3, 8, 32, 384),
    rzout=spec(BF, 3, 4, 32, 256),
    rygu=spec(BF, 3, 4, 2, 32, 768),
    rzdn=spec(BF, 3, 4, 96, 256),
    sqkv=spec(BF, 8, 32, 384),
    sout=spec(BF, 4, 32, 256),
    sgu=spec(BF, 4, 2, 32, 768),
    sdn=spec(BF, 4, 96, 256),
    fqkv=spec(BF, 8, 32, 384),
    fout=spec(BF, 4, 32, 256),
    fgu=spec(BF, 8, 32, 768),
    fdn=spec(BF, 4, 96, 256),
)
SUB = dict(
    a=spec(BF, 8, 32, 1024),
    h=spec(BF, 32, 1024),
    gr=spec(BF, 32, 1024),
    gb=spec(BF, 8, 32, 1024),
)
EXCHANGE = dict(
    pb=spec(BF, 2, 4, 32, 1024),
    sib=spec(BF, 4, 32, 1024),
    xs=spec(BF, 3, 32, 1024),
    xr=spec(BF, 3, 32, 1024),
)
N_SEM = 480
N_LAYERS, N_SUB, N_EXCHANGE = 2, 4, 8


def groups():
    arguments = [(0, 0, COMMON_IN)] + [(1, l, LAYER_IN) for l in range(N_LAYERS)]
    results = [(0, 0, COMMON_OUT)] + [(1, l, LAYER_OUT) for l in range(N_LAYERS)]
    scratch = [(0, 0, COMMON)] + [(1, l, LAYER) for l in range(N_LAYERS)]
    scratch += [(2, i, SUB) for i in range(N_SUB)] + [(3, n, EXCHANGE) for n in range(N_EXCHANGE)]
    return arguments, results, scratch


def named(refs):
    spaces = [[SimpleNamespace() for _ in range(n)] for n in (1, N_LAYERS, N_SUB, N_EXCHANGE)]
    left = list(refs)
    for group in groups():
        for kind, index, specs in group:
            for name in specs:
                setattr(spaces[kind][index], name, left.pop(0))
    return spaces[0][0], spaces[1], spaces[2], spaces[3]


def specs_of(group):
    return [entry for _, _, specs in group for entry in specs.values()]


def nn(a, b):
    return lax.dot_general(a, b, (((1,), (0,)), ((), ())), preferred_element_type=F32)


def nt(a, b):
    return lax.dot_general(a, b, (((1,), (1,)), ((), ())), preferred_element_type=F32)


def tn(a, b):
    return lax.dot_general(a, b, (((0,), (0,)), ((), ())), preferred_element_type=F32)


def normalize(h):
    inverse = lax.rsqrt(jnp.mean(h * h, axis=-1, keepdims=True) + EPS)
    return h * inverse, inverse


def kernel(*refs):
    R, L, S, X = named(refs[:-1])
    sems = refs[-1]
    used = [0]
    pending = []

    def new():
        used[0] += 1
        return sems.at[used[0] - 1]

    x = lax.axis_index("section")
    c = lax.axis_index("ctx")
    z, y, k = lax.div(c, 8), lax.rem(lax.div(c, 2), 4), lax.rem(c, 2)
    t = 2 * x + k
    s = lax.div(y, 2)
    yy = lax.rem(y, 2)
    other = 1 - k

    def plus(v, j):
        return lax.rem(v + j, 4)

    def dev(xd, zd, yd, kd):
        return {"section": xd, "ctx": zd * 8 + yd * 2 + kd}

    def flip(j):
        return k if j % 2 == 0 else other

    sibling = dev(x, z, y, other)

    def put(src, dst, to, rsem):
        copy = pltpu.make_async_remote_copy(
            src_ref=src, dst_ref=dst, send_sem=new(), recv_sem=rsem, device_id=to, device_id_type=MESH
        )
        copy.start()
        pending.append((None, copy))

    def put_or_keep(mine, src, dst, to, rsem):
        copy = pltpu.make_async_remote_copy(
            src_ref=src, dst_ref=dst, send_sem=new(), recv_sem=rsem, device_id=to, device_id_type=MESH
        )

        @pl.when(mine)
        def _():
            pltpu.make_async_copy(src, dst, rsem).start()

        @pl.when(jnp.logical_not(mine))
        def _():
            copy.start()

        pending.append((mine, copy))

    def arrived(ref, sem):
        pltpu.make_async_copy(ref, ref, sem).wait()

    barrier = pltpu.get_barrier_semaphore()

    def greet(d):
        pl.semaphore_signal(barrier, inc=1, device_id=d, device_id_type=MESH)

    count = 0
    for j in range(4):
        for i in range(2):
            if (j, i) != (0, 0):
                greet(dev(plus(x, j), z, y, flip(i)))
                count += 1
            if j:
                greet(dev(x, z, plus(y, j), flip(i)))
                greet(dev(x, plus(z, j), y, flip(i)))
                count += 2
            greet(dev(plus(x, j), 3 - z, 3 - y, flip(i)))
            count += 1
    crossing = jnp.where(x == z, 0, 1)

    @pl.when(x != z)
    def _():
        for j in range(4):
            for i in range(2):
                greet(dev(z, x, plus(y, j), flip(i)))

    pl.semaphore_wait(barrier, count + 8 * crossing)

    W = [SimpleNamespace(), SimpleNamespace()]

    def weights_att_first(l):
        wst = L[l].wst
        for i in range(2):
            for n, w in enumerate((L[l].wq, L[l].wk, L[l].wv)):
                wst[i, :, 128 * n : 128 * n + 128] = w[:, 128 * i : 128 * i + 128]
        w = L[l].wqkv
        sem = W[l].q1 = new()
        pltpu.make_async_copy(wst.at[k], w.at[z, 2 * y + k], sem).start()
        for j in range(1, 8):
            put(wst.at[flip(j)], w.at[z, 2 * y + k], dev(x, z, plus(y, j // 2), flip(j)), sem)
        wo, w = L[l].wo, L[l].wout
        sem = W[l].o1 = new()
        crossed(wo, w, sem)

    def crossed(src, w, sem):
        slot = w.at[x, 2 * yy + k]
        mine = (x == z) & (s == k)
        put_or_keep(mine, src, slot, dev(z, x, y, s), sem)
        for j in range(1, 4):
            put(src, slot, dev(z, x, plus(y, j), s), sem)

    def weights_ff_first(l):
        src, w = L[l].gus, L[l].wgu
        sem = W[l].g1 = new()
        pltpu.make_async_copy(src.at[k], w.at[z, y, k], sem).start()
        for j in range(1, 8):
            put(src.at[flip(j)], w.at[z, y, k], dev(x, plus(z, j // 2), y, flip(j)), sem)
        wds = L[l].wds
        wds[0:88, :] = L[l].wd[...]
        wds[88:96, :] = jnp.zeros((8, 256), BF)
        sem = W[l].d1 = new()
        crossed(wds, L[l].wdn, sem)

    def along_z(w):
        sem = new()
        for j in (1, 3, 2):
            put(w.at[z], w.at[z], dev(x, plus(z, j), y, k), sem)
        return sem

    def weights_att_second(l):
        w, wo = L[l].wqkv, L[l].wout
        arrived(w.at[z], W[l].q1)
        W[l].q2 = along_z(w)
        arrived(wo.at[z], W[l].o1)
        W[l].o2 = along_z(wo)

    def weights_ff_second(l):
        w, wd = L[l].wgu, L[l].wdn
        arrived(w.at[z], W[l].g1)
        sem = W[l].g2 = new()
        for j in (1, 3, 2):
            put(w.at[:, y], w.at[:, y], dev(x, z, plus(y, j), k), sem)
        arrived(wd.at[z], W[l].d1)
        W[l].d2 = along_z(wd)

    def rs_start(n, part):
        pb, sib = X[n].pb, X[n].sib
        for i in range(8):
            pb[i % 2, i // 2] = part[32 * i : 32 * i + 32].astype(BF)
        sem = [new() for _ in range(4)]
        for j in (1, 3, 2, 0):
            xd = plus(x, j)
            put(pb.at[other, xd], sib.at[xd], sibling, sem[j])
        return sem

    def rs_mid(n, sem):
        pb, sib, xs, xr = X[n].pb, X[n].sib, X[n].xs, X[n].xr
        out = []
        for j in (1, 3, 2):
            xd = plus(x, j)
            arrived(sib.at[xd], sem[j])
            xs[j - 1] = (pb[k, xd].astype(F32) + sib[xd].astype(F32)).astype(BF)
            out.append(new())
            put(xs.at[j - 1], xr.at[j - 1], dev(xd, z, y, k), out[-1])
        return sem[0], out

    def rs_end(n, sems_):
        pb, sib, xr = X[n].pb, X[n].sib, X[n].xr
        own, out = sems_
        arrived(sib.at[x], own)
        total = pb[k, x].astype(F32) + sib[x].astype(F32)
        for j, sem in zip((1, 3, 2), out):
            arrived(xr.at[j - 1], sem)
            total += xr[j - 1].astype(F32)
        return total

    def gather(buf, block):
        buf[t] = block
        rx = [new() for _ in range(4)]
        rk = [new() for _ in range(4)]
        for j in (1, 3, 2):
            put(buf.at[t], buf.at[t], dev(plus(x, j), z, y, k), rx[j])
        put(buf.at[t], buf.at[t], sibling, rk[0])
        for j in (1, 3, 2):
            slot = buf.at[2 * plus(x, 4 - j) + k]
            arrived(slot, rx[j])
            put(slot, slot, sibling, rk[j])
        for j in range(4):
            arrived(buf.at[0], rk[j])

    def to_owners(rows, stage, landing):
        for i in range(4):
            stage[i] = rows[:, 256 * i : 256 * i + 256]
        near = x < 2
        zd, yd = jnp.where(near, z, 3 - z), jnp.where(near, y, 3 - y)
        kd = lax.rem(x, 2)
        sem = new()
        put_or_keep(near & (kd == k), stage.at[x], landing.at[s, k], dev(x, zd, yd, kd), sem)
        for j in range(1, 4):
            xd = plus(x, j)
            put(stage.at[xd], landing.at[s, k], dev(xd, zd, yd, kd), sem)
        return sem

    def spread_tokens(src, dst):
        sem = new()
        near, far = pl.ds(2 * k, 2), pl.ds(4 + 2 * k, 2)
        dst[near] = src[s]
        put(src.at[s], dst.at[near], sibling, sem)
        put(src.at[1 - s], dst.at[far], dev(x, 3 - z, 3 - y, k), sem)
        put(src.at[1 - s], dst.at[far], dev(x, 3 - z, 3 - y, other), sem)
        return sem

    lane = lax.rem(lax.broadcasted_iota(I32, (1, 512), 1), 256)
    own_block = 4 * z + y
    query_pos = jnp.where(lane < 128, 128 * own_block + lane, 128 * (15 - own_block) + lane - 128)
    query_start = R.startq[0:1, :]
    head_lane = lax.broadcasted_iota(I32, (256, 128), 1) < 64

    def two_heads(v):
        zero = jnp.zeros_like(v)
        return jnp.concatenate([jnp.where(head_lane, v, zero), jnp.where(head_lane, zero, v)], axis=0)

    def own_heads(vt):
        return jnp.concatenate([vt[0:64, 0:256], vt[64:128, 256:512]], axis=0)

    def gain_row(i):
        return R.gains[i : i + 1, :]

    def full(ref):
        return ref[...].reshape(256, 1024)

    def keys_of(l, zz):
        return L[l].kv[zz, :, :, 0:128].reshape(512, 128)

    def values_of(l, zz):
        return L[l].kv[zz, :, :, 128:256].reshape(512, 128)

    def attention_forward(l, hook):
        arrived(L[l].wqkv.at[0:3], W[l].q2)
        qkv = nn(full(S[2 * l].a), L[l].wqkv[...].reshape(1024, 384))
        q = (qkv[:, 0:128].astype(BF) * 0.125).astype(BF)
        keys = qkv[:, 128:256].astype(BF)
        u = qkv[:, 256:384]
        if l == 0:
            values = u.astype(BF)
        else:
            values = (0.5 * u + 0.5 * L[0].kv[z, yy, :, 128:256].astype(F32)).astype(BF)
        kv = L[l].kv
        kv[z, yy, :, 0:128] = keys
        kv[z, yy, :, 128:256] = values
        q2 = two_heads(q)
        L[l].q2[...] = q2
        sem = new()
        put(kv.at[z, yy], kv.at[z, yy], dev(x, z, y + 1 - 2 * yy, k), sem)
        arrived(kv.at[z, yy], sem)
        zsem = [new() for _ in range(4)]
        for j in (1, 3, 2):
            put(kv.at[z], kv.at[z], dev(x, plus(z, j), y, k), zsem[j])
        hook()
        scores = R.scores
        top = jnp.full((1, 512), MASKED, F32)
        for j in (0, 3, 1, 2):
            zz = plus(z, j)
            if j:
                arrived(kv.at[zz], zsem[4 - j])
            scores[4 * j : 4 * j + 4] = nt(keys_of(l, zz), L[l].q2[...]).reshape(4, 128, 512)

            def mask(i, top, j=j, zz=zz):
                block = 4 * zz + 2 * s + lax.div(i, 2)
                base = 128 * (block + lax.rem(i, 2) * (15 - 2 * block))
                row = lax.broadcasted_iota(I32, (128, 512), 0)
                seen = (row >= query_start - base) & (row <= query_pos - base)
                v = jnp.where(seen, scores[4 * j + i], MASKED)
                scores[4 * j + i] = v
                return jnp.maximum(top, jnp.max(v, axis=0, keepdims=True))

            top = lax.fori_loop(0, 4, mask, top)

        def expo(i, total):
            v = jnp.exp(scores[i] - top)
            scores[i] = v
            return total + jnp.sum(v, axis=0, keepdims=True)

        total = lax.fori_loop(0, 16, expo, jnp.zeros((1, 512), F32))
        share = 1.0 / total
        prob = L[l].prob

        def norm(i, carry):
            prob[i] = (scores[i] * share).astype(BF)
            return carry

        lax.fori_loop(0, 16, norm, 0)
        ot = jnp.zeros((128, 512), F32)
        for j in range(4):
            ot += tn(values_of(l, plus(z, j)), prob[4 * j : 4 * j + 4].reshape(512, 512))
        ot = own_heads(ot)
        L[l].ot[...] = ot
        o = jnp.transpose(ot).astype(BF)
        arrived(L[l].wout.at[0:3], W[l].o2)
        return jnp.concatenate([nn(o, L[l].wout[i].reshape(128, 256)) for i in range(4)], axis=1)

    def feedforward_forward(l, hook):
        arrived(L[l].wgu.at[0:3], W[l].g2)
        gu = nn(full(S[2 * l + 1].a), L[l].wgu[...].reshape(1024, 768))
        L[l].gu[...] = gu
        gate, up = gu[:, 0:384], gu[:, 384:768]
        hidden = (gate * jax.nn.sigmoid(gate) * up).astype(BF)
        L[l].hid[...] = hidden
        hook()
        arrived(L[l].wdn.at[0:3], W[l].d2)
        return jnp.concatenate([nn(hidden, L[l].wdn[i].reshape(384, 256)) for i in range(4)], axis=1)

    def next_rows(i, part):
        total = rs_end(i, rs_mid(i, rs_start(i, part)))
        rows = (S[i].h[...].astype(F32) + total).astype(BF)
        S[i + 1].h[...] = rows
        normed, _ = normalize(rows.astype(F32))
        gather(S[i + 1].a, (normed * gain_row(i + 1)).astype(BF))

    def norm_backward(i, da):
        normed, inverse = normalize(S[i].h[...].astype(F32))
        R.gg[i : i + 1, :] = jnp.sum(da * normed, axis=0, keepdims=True)
        scaled = da * gain_row(i)
        mixed = scaled - normed * jnp.mean(scaled * normed, axis=-1, keepdims=True)
        return (S[i].gr[...].astype(F32) + inverse * mixed).astype(BF)

    G = [SimpleNamespace(), SimpleNamespace()]

    def send_z(g, landing):
        sem = new()
        for j in (1, 3, 2):
            zd = plus(z, j)
            put(g.at[zd], landing.at[j - 1], dev(x, zd, y, k), sem)
        return sem

    def attention_backward(l, hook1, hook2):
        i0 = 2 * l
        gb = full(S[i0].gb)
        wo = L[l].wout
        dot_ = nt(wo[0].reshape(128, 256), gb[:, 0:256])
        for i in range(1, 4):
            dot_ += nt(wo[i].reshape(128, 256), gb[:, 256 * i : 256 * i + 256])
        dot_ = dot_.astype(BF).astype(F32)
        do2 = two_heads(jnp.transpose(dot_).astype(BF))
        prod = dot_ * L[l].ot[...]
        delta = jnp.concatenate(
            [jnp.sum(prod[0:64], axis=0, keepdims=True), jnp.sum(prod[64:128], axis=0, keepdims=True)], axis=1
        )
        dkv, prob = L[l].dkv, L[l].prob
        dq = jnp.zeros((128, 512), F32)
        zsem = G[l].kv = new()
        for j in (1, 3, 2, 0):
            zz = plus(z, j)
            p = prob[4 * j : 4 * j + 4].reshape(512, 512)
            dp = nt(values_of(l, zz), do2)
            ds = (p.astype(F32) * (dp - delta)).astype(BF)
            dkv[zz, :, :, 0:128] = nn(ds, L[l].q2[...]).astype(BF).reshape(2, 256, 128)
            dkv[zz, :, :, 128:256] = nn(p, do2).astype(BF).reshape(2, 256, 128)
            if j:
                put(dkv.at[zz], L[l].dkvr.at[j - 1], dev(x, zz, y, k), zsem)
            dq += tn(keys_of(l, zz), ds)
        dq = jnp.transpose(own_heads(dq) * 0.125).astype(BF)
        hook1()
        got = L[l].dkvr
        arrived(got, zsem)
        tot = dkv[z].astype(F32) + got[0].astype(F32) + got[1].astype(F32) + got[2].astype(F32)
        R.dkvf[...] = tot
        mate = 1 - yy
        L[l].dkvs[...] = R.dkvf[mate].astype(BF)
        sem = new()
        put(L[l].dkvs, L[l].dkvy, dev(x, z, y + 1 - 2 * yy, k), sem)
        arrived(L[l].dkvy, sem)
        tot = R.dkvf[yy] + L[l].dkvy[...].astype(F32)
        dk = tot[:, 0:128].astype(BF)
        dvals = tot[:, 128:256]
        if l == 1:
            half = 0.5 * dvals.astype(BF).astype(F32)
            du = half.astype(BF)
            R.dmh[...] = du
        else:
            du = (dvals + R.dmh[...].astype(F32)).astype(BF)
        dqkv = jnp.concatenate([dq, dk, du], axis=1)
        rs = rs_start(4 + i0, nt(dqkv, L[l].wqkv[...].reshape(1024, 384)))
        rs = rs_mid(4 + i0, rs)
        at = jnp.transpose(full(S[i0].a))
        gw = L[l].gwqkv
        gw[...] = nn(at, dqkv).astype(BF).reshape(4, 8, 32, 384)
        G[l].q = send_z(gw, L[l].rzqkv)
        otb = L[l].ot[...].astype(BF)
        gw = L[l].gwout
        for i in range(4):
            gw[i] = nn(otb, gb[:, 256 * i : 256 * i + 256]).astype(BF).reshape(4, 32, 256)
        G[l].o = send_z(gw, L[l].rzout)
        hook2()
        return norm_backward(i0, rs_end(4 + i0, rs))

    def feedforward_backward(l, hook1, hook2):
        i0 = 2 * l + 1
        gb = full(S[i0].gb)
        wd = L[l].wdn
        dhid = nt(gb[:, 0:256], wd[0].reshape(384, 256))
        for i in range(1, 4):
            dhid += nt(gb[:, 256 * i : 256 * i + 256], wd[i].reshape(384, 256))
        gu = L[l].gu[...]
        gate, up = gu[:, 0:384], gu[:, 384:768]
        sig = jax.nn.sigmoid(gate)
        dgate = dhid * up * sig * (1.0 + gate * (1.0 - sig))
        dup = dhid * (gate * sig)
        dgu = jnp.concatenate([dgate.astype(BF), dup.astype(BF)], axis=1)
        rs = rs_start(4 + i0, nt(dgu, L[l].wgu[...].reshape(1024, 768)))
        hook1()
        rs = rs_mid(4 + i0, rs)
        at = jnp.transpose(full(S[i0].a))
        gw = L[l].gwgu
        gw[...] = nn(at, dgu).astype(BF).reshape(4, 4, 2, 32, 768)
        sem = G[l].g = new()
        for j in (1, 3, 2):
            yd = plus(y, j)
            put(gw.at[:, yd], L[l].rygu.at[j - 1], dev(x, z, yd, k), sem)
        ht = jnp.transpose(L[l].hid[...])
        gw = L[l].gwdn
        for i in range(4):
            gw[i] = nn(ht, gb[:, 256 * i : 256 * i + 256]).astype(BF).reshape(4, 96, 256)
        G[l].d = send_z(gw, L[l].rzdn)
        hook2()
        return norm_backward(i0, rs_end(4 + i0, rs))

    def summed(own, got):
        return own.astype(F32) + got[0].astype(F32) + got[1].astype(F32) + got[2].astype(F32)

    def owners_crossed(src, landing):
        sem = new()
        first = 2 * yy + k
        for j in range(4):
            m = plus(first, j)
            to = dev(z, x, 2 * k + lax.div(m, 2), lax.rem(m, 2))
            if j == 0:
                put_or_keep((x == z) & (s == k), src.at[m], landing.at[y], to, sem)
            else:
                put(src.at[m], landing.at[y], to, sem)
        return sem

    def grads_att_second(l):
        gw, got, st, land = L[l].gwqkv, L[l].rzqkv, L[l].sqkv, L[l].fqkv
        arrived(got, G[l].q)
        st[...] = summed(gw[z], got).astype(BF)
        sem = G[l].q2 = new()
        land[0] = st[2 * y + k]
        for j in range(1, 8):
            yd, kd = plus(y, j // 2), flip(j)
            put(st.at[2 * yd + kd], land.at[j], dev(x, z, yd, kd), sem)
        gw, got, st = L[l].gwout, L[l].rzout, L[l].sout
        arrived(got, G[l].o)
        st[...] = summed(gw[z], got).astype(BF)
        G[l].o2 = owners_crossed(st, L[l].fout)

    def halves(land):
        own = land[0].astype(F32) + land[2].astype(F32) + land[4].astype(F32) + land[6].astype(F32)
        far = land[1].astype(F32) + land[3].astype(F32) + land[5].astype(F32) + land[7].astype(F32)
        return own, far

    def four(land):
        return land[0].astype(F32) + land[1].astype(F32) + land[2].astype(F32) + land[3].astype(F32)

    def grads_att_end(l):
        land = L[l].fqkv
        arrived(land.at[1:8], G[l].q2)
        own, far = halves(land)
        first = k == 0
        low, high = jnp.where(first, own, far), jnp.where(first, far, own)
        for n, result in enumerate((L[l].oq, L[l].ok, L[l].ov)):
            result[:, 0:128] = low[:, 128 * n : 128 * n + 128]
            result[:, 128:256] = high[:, 128 * n : 128 * n + 128]
        land = L[l].fout
        arrived(land, G[l].o2)
        L[l].oo[...] = four(land)

    def grads_ff_second(l):
        gw, got, st, land = L[l].gwgu, L[l].rygu, L[l].sgu, L[l].fgu
        arrived(got, G[l].g)
        for i in range(4):
            st[i] = (
                gw[i, y].astype(F32) + got[0, i].astype(F32) + got[1, i].astype(F32) + got[2, i].astype(F32)
            ).astype(BF)
        sem = G[l].g2 = new()
        land[0] = st[z, k]
        for j in range(1, 8):
            zd, kd = plus(z, j // 2), flip(j)
            put(st.at[zd, kd], land.at[j], dev(x, zd, y, kd), sem)
        gw, got, st = L[l].gwdn, L[l].rzdn, L[l].sdn
        arrived(got, G[l].d)
        st[...] = summed(gw[z], got).astype(BF)
        G[l].d2 = owners_crossed(st, L[l].fdn)

    def grads_ff_end(l):
        land = L[l].fgu
        arrived(land.at[1:8], G[l].g2)
        own, far = halves(land)
        L[l].ogu[k] = own
        L[l].ogu[other] = far
        land = L[l].fdn
        arrived(land, G[l].d2)
        L[l].od[...] = four(land)

    def nothing():
        pass

    weights_att_first(0)
    in_sem = spread_tokens(R.xin, R.hin)
    gx_sem = new()
    for j in (1, 3, 2):
        put(R.gst, R.gx.at[j - 1], dev(plus(x, j), z, y, k), gx_sem)
    weights_ff_first(0)
    arrived(R.gx, gx_sem)
    R.g1[...] = R.gst[...] + R.gx[0] + R.gx[1] + R.gx[2]
    gy_sem = new()
    R.gyr[2 * y + k] = R.g1[...]
    for j in range(1, 8):
        put(R.g1, R.gyr.at[2 * y + k], dev(x, z, plus(y, j // 2), flip(j)), gy_sem)
    weights_att_second(0)
    arrived(R.gyr.at[0:7], gy_sem)
    for i in range(2):
        R.gz[z, i] = R.gyr[4 * i] + R.gyr[4 * i + 1] + R.gyr[4 * i + 2] + R.gyr[4 * i + 3]
    gz_sem = new()
    for j in (1, 3, 2):
        put(R.gz.at[z], R.gz.at[z], dev(x, plus(z, j), y, k), gz_sem)
    R.gg[...] = jnp.zeros((8, 1024), F32)
    arrived(R.hin.at[0:6], in_sem)
    arrived(R.gz.at[0:3], gz_sem)
    R.gains[...] = jnp.concatenate([R.gz[i // 2, i % 2] for i in range(8)], axis=1)
    normed, _ = normalize(full(R.hin).astype(F32))
    S[0].a[...] = (normed * gain_row(0)).astype(BF).reshape(8, 32, 1024)
    S[0].h[...] = R.hin[t]
    cot_sem = []

    def after_keys_0():
        weights_ff_second(0)
        weights_att_first(1)
        weights_ff_first(1)

    def after_keys_1():
        weights_ff_second(1)
        cot_sem.append(spread_tokens(R.cot, S[3].gb))

    next_rows(0, attention_forward(0, after_keys_0))
    next_rows(1, feedforward_forward(0, lambda: weights_att_second(1)))
    next_rows(2, attention_forward(1, after_keys_1))
    last = rs_mid(3, rs_start(3, feedforward_forward(1, nothing)))
    arrived(S[3].gb.at[0:6], cot_sem[0])
    S[3].gr[...] = S[3].gb[t]
    out_sem = []

    def finish_outputs():
        rows = (S[3].h[...].astype(F32) + rs_end(3, last)).astype(BF)
        out_sem.append(to_owners(rows, R.outst, R.outrv))

    def hand_back(i, rows):
        S[i].gr[...] = rows
        gather(S[i].gb, rows)

    hand_back(2, feedforward_backward(1, finish_outputs, nothing))
    hand_back(1, attention_backward(1, lambda: grads_ff_second(1), nothing))
    hand_back(0, feedforward_backward(0, lambda: grads_att_second(1), lambda: grads_ff_end(1)))
    rows = attention_backward(0, lambda: grads_ff_second(0), lambda: grads_att_end(1))
    in_grad_sem = to_owners(rows, R.ingst, R.ingrv)
    gg_sem = new()
    for j in (1, 3, 2):
        put(R.gg, R.ggx.at[j - 1], dev(plus(x, j), z, y, k), gg_sem)
    grads_att_second(0)
    arrived(R.ggx, gg_sem)
    gg = R.gg[...] + R.ggx[0] + R.ggx[1] + R.ggx[2]
    for i in range(4):
        R.ggz[i] = gg[:, 256 * i : 256 * i + 256]
    gg_sem = new()
    for j in (1, 3, 2):
        zd = plus(z, j)
        put(R.ggz.at[zd], R.ggzr.at[j - 1], dev(x, zd, y, k), gg_sem)
    grads_ff_end(0)
    arrived(R.outrv, out_sem[0])
    R.out[...] = R.outrv[...]
    arrived(R.ggzr, gg_sem)
    gg = R.ggz[z] + R.ggzr[0] + R.ggzr[1] + R.ggzr[2]
    R.ggy[0] = gg[:, 0:128]
    R.ggy[1] = gg[:, 128:256]
    gg_sem = new()
    R.ggyr[0] = R.ggy[s]
    for j in range(1, 8):
        yd = plus(y, j // 2)
        put(R.ggy.at[lax.div(yd, 2)], R.ggyr.at[j], dev(x, z, yd, flip(j)), gg_sem)
    arrived(R.ingrv, in_grad_sem)
    R.ing[...] = R.ingrv[...]
    arrived(R.ggyr.at[1:8], gg_sem)
    gg = R.ggyr[0]
    for j in range(1, 8):
        gg = gg + R.ggyr[j]
    R.ogg[...] = gg
    grads_att_end(0)
    for mine, copy in pending:
        if mine is None:
            copy.wait_send()
        else:

            @pl.when(jnp.logical_not(mine))
            def _(copy=copy):
                copy.wait_send()

    assert used[0] <= N_SEM, used


def call(*args):
    whole = pl.BlockSpec(memory_space=pltpu.VMEM)
    arguments, results, scratch = (specs_of(group) for group in groups())
    return pl.pallas_call(
        kernel,
        out_shape=[jax.ShapeDtypeStruct(shape, dtype) for shape, dtype in results],
        in_specs=[whole] * len(arguments),
        out_specs=[whole] * len(results),
        scratch_shapes=[pltpu.VMEM(shape, dtype) for shape, dtype in scratch]
        + [pltpu.SemaphoreType.DMA((N_SEM,))],
        compiler_params=pltpu.CompilerParams(
            collective_id=0, has_side_effects=True, vmem_limit_bytes=62 * 1024 * 1024
        ),
    )(*args)


def packed(w):
    rows = w.shape[0]
    groups = w.reshape(rows, 2, 4, 88)
    return jnp.pad(groups, ((0, 0), (0, 0), (0, 0), (0, 8))).reshape(rows, 2, 384).swapaxes(0, 1)


def unpacked(g):
    rows = g.shape[1]
    return g.swapaxes(0, 1).reshape(rows, 2, 4, 96)[..., :88].reshape(rows, 704)


def body(inputs, cotangent, segment_ids, gains, *weights):
    x = lax.axis_index("section")
    c = lax.axis_index("ctx")
    z, y = c // 8, (c // 2) % 4
    segments = lax.dynamic_index_in_dim(segment_ids.reshape(2, 2048), y // 2, 0, keepdims=False)
    first = jnp.sum(segments == 0).astype(I32)
    second = jnp.sum(segments <= 1).astype(I32)
    row = jnp.arange(512, dtype=I32) % 256
    block = 4 * z + y
    pos = jnp.where(row < 128, 128 * block + row, 128 * (15 - block) + row - 128)
    start = jnp.where(pos < first, 0, jnp.where(pos < second, first, second)).astype(I32)
    startq = jnp.broadcast_to(start[None], (8, 512))
    at_row = lax.broadcasted_iota(I32, (8, 128), 0) == x
    at_lane = lax.broadcasted_iota(I32, (8, 128), 1) // 32 == c % 4
    piece = jnp.tile(gains.astype(F32), (1, 4))
    gst = jnp.where(at_row & at_lane, piece, 0.0)
    args = [inputs.reshape(2, 2, 32, 1024), cotangent.reshape(2, 2, 32, 1024), gst, startq]
    for l in range(2):
        wq, wk, wv, wo, wg, wu, wd = weights[7 * l : 7 * l + 7]
        args += [wq, wk, wv, wo, jnp.concatenate([packed(wg), packed(wu)], axis=2), wd]
    outs = call(*args)
    out, ing, ogg = outs[:3]
    gain = lax.dynamic_slice(ogg, (x, (c % 4) * 32), (1, 32))
    results = [out.reshape(2, 1, 64, 256), ing.reshape(2, 1, 64, 256), gain]
    for l in range(2):
        oq, ok, ov, oo, ogu, od = outs[3 + 6 * l : 9 + 6 * l]
        results += [oq, ok, ov, oo, unpacked(ogu[:, :, :384]), unpacked(ogu[:, :, 384:])]
        results += [od[:88]]
    return tuple(results)


def solution(mesh):
    tokens = P(None, None, "ctx", None)
    weight = P("ctx", "section")
    return jax.shard_map(
        body,
        mesh=mesh,
        in_specs=(tokens, tokens, P(), P("section", "ctx")) + (weight,) * 14,
        out_specs=(P(None, None, "ctx", "section"),) * 2 + (P("section", "ctx"),) + (weight,) * 14,
        check_vma=False,
    )
```

profile of v0, /device:TPU:4, one launch (start us, length us, event | category | flops | bytes accessed | tf_op | source)
XLA Modules:
  0.0 292.3 jit_solution(17844579014073702431)
XLA Ops:
  0.7 0.0 copy-start.18
  0.7 0.0 copy-start.17
  0.7 0.0 copy-start.5
  0.8 0.6 copy-done.18
  1.4 0.1 copy-done.17
  1.5 0.7 fusion
  2.1 1.3 select_select_fusion
  3.4 0.1 tile.16
  3.5 0.7 fusion.3.refs_2_
  4.2 0.6 broadcast_in_dim.26.refs_3_
  4.8 0.0 copy-done.5
  4.8 0.1 reshape.130
  5.0 0.0 copy-start.6
  5.0 0.1 reshape.131
  5.1 0.7 copy-done.6
  5.8 0.1 reshape.132
  6.0 0.0 copy-start.7
  6.0 0.1 reshape.133
  6.1 0.7 copy-done.7
  6.8 0.1 reshape.134
  7.0 0.0 copy-start.8
  7.0 0.1 reshape.135
  7.1 0.7 copy-done.8
  7.8 0.1 reshape.136
  8.0 0.1 reshape.137
  8.1 0.7 pad_maximum_fusion
  8.8 268.3 %shard_map.305 = (bf16[2,2,32,256]{3,2,1,0:T(8,128)(2,1)}, bf16[2,2,32,256]{3,2,1,0:T(8,128)(2,1)}, f32[8,128]{1,0:T(8,128)}, f32[32,256]{1,0:T(8,128)}, f32[32,...) custom-call(bf16[2,2,32,1024]{3,2,1,0:T(8,128)(2,1)} %bitcast.47, ...), custom_call_target="tpu_custom_call" | custom-call | tf_op jit(solution)/shard_map/pallas_call | solution.py:757
  277.2 0.0 copy-start.2
  277.2 0.0 copy-start.1
  277.2 1.3 dynamic_slice.8
  278.5 1.5 slice.34
  280.0 0.0 copy-done.2
  280.0 0.6 slice.39
  280.7 0.0 copy-done.1
  280.7 0.1 reshape.142
  280.9 0.8 reshape.143
  281.6 0.1 reshape.140
  281.8 0.0 copy-start
  281.8 0.8 reshape.141
  282.6 0.1 copy-done
  282.7 0.1 reshape.146
  282.9 0.8 reshape.147
  283.6 0.1 reshape.144
  283.8 0.8 reshape.145
  284.6 0.1 copy-done.4
  284.7 0.6 copy.55
  285.3 0.2 copy-done.3
  285.5 0.6 copy.56
  286.1 0.1 copy-done.16
  286.3 0.6 copy.57
  286.9 0.2 copy-done.15
  287.0 0.6 copy.58
  287.7 0.2 copy-done.14
  287.8 0.6 copy.59
  288.4 0.2 copy-done.13
  288.6 0.6 copy.60
  289.2 0.2 copy-done.12
  289.4 0.6 copy.61
  290.0 0.2 copy-done.11
  290.1 0.6 copy.62
  290.7 0.2 copy-done.10
  290.9 0.6 copy.63
  291.5 0.2 copy-done.9
  291.7 0.6 copy.64
  (29 shorter events, 0.4 us)
Async XLA Ops:
  0.7 0.7 copy-start.18
  0.7 0.7 copy-start.17
  0.7 4.1 %copy-start.5 = (bf16[32,704]{1,0:T(8,128)(2,1)S(1)}, bf16[32,704]{1,0:T(8,128)(2,1)}, u32[]{:S(2)}) copy-start(bf16[32,704]{1,0:T(8,128)(2,1)} %param.26) | copy-start | bytes 135172
  5.0 0.8 copy-start.6
  6.0 0.8 copy-start.7
  7.0 0.8 copy-start.8
  277.2 2.9 copy-start.2
  277.2 3.5 %copy-start.1 = (f32[2,32,768]{2,1,0:T(8,128)S(1)}, f32[2,32,768]{2,1,0:T(8,128)}, u32[]{:S(2)}) copy-start(f32[2,32,768]{2,1,0:T(8,128)} %get-tuple-element.39) | copy-start | bytes 589828
  281.8 0.9 copy-start
  283.8 0.8 copy-start.4
  284.6 0.9 copy-start.3
  285.5 0.8 copy-start.16
  286.3 0.8 copy-start.15
  287.0 0.8 copy-start.14
  287.8 0.8 copy-start.13
  288.6 0.8 copy-start.12
  289.4 0.8 copy-start.11
  290.1 0.8 copy-start.10
  290.9 0.8 copy-start.9
where the time goes:
time: 296 us; the launch traced here: 292 us
  Pallas kernels  268 us (91%)
  local copies, waits for them, and re-layouts  19.5 us (7%)
  other arithmetic  3.33 us (1%)
    pallas_call x1, Pallas kernels, call(): pl.pallas_call(kernel, out_shape=[jax.ShapeDtypeStruct(shape, dtype) for...  268 us
    unnamed x48, local copies, waits for them, and re-layouts  10.5 us

commit v1 on v0

v1 whole, which is shorter than its diff:
```python
from types import SimpleNamespace

import jax
import jax.numpy as jnp
from jax import lax
from jax.experimental import pallas as pl
from jax.experimental.pallas import tpu as pltpu
from jax.sharding import PartitionSpec as P

MESH = pl.DeviceIdType.MESH
BF = jnp.bfloat16
F32 = jnp.float32
I32 = jnp.int32
EPS = 1e-06
MASKED = -1e30


def spec(dtype, *shape):
    return shape, dtype


LAYER_IN = dict(
    wq=spec(BF, 32, 256),
    wk=spec(BF, 32, 256),
    wv=spec(BF, 32, 256),
    wo=spec(BF, 32, 256),
    wg=spec(BF, 32, 704),
    wu=spec(BF, 32, 704),
    wd=spec(BF, 88, 256),
)
COMMON_IN = dict(
    xin=spec(BF, 2, 2, 32, 1024), cot=spec(BF, 2, 2, 32, 1024), seg=spec(I32, 2, 1, 2048), gains_in=spec(BF, 1, 32)
)
LAYER_OUT = dict(
    oq=spec(F32, 32, 256),
    ok=spec(F32, 32, 256),
    ov=spec(F32, 32, 256),
    oo=spec(F32, 32, 256),
    og=spec(F32, 32, 704),
    ou=spec(F32, 32, 704),
    od=spec(F32, 88, 256),
)
COMMON_OUT = dict(out=spec(BF, 2, 1, 64, 256), ing=spec(BF, 2, 1, 64, 256), ogg=spec(F32, 1, 32))
COMMON = dict(
    hin=spec(BF, 8, 32, 1024),
    pick=spec(BF, 704, 768),
    gst=spec(F32, 8, 128),
    gx=spec(F32, 3, 8, 128),
    g1=spec(F32, 8, 128),
    gyr=spec(F32, 8, 8, 128),
    gz=spec(F32, 4, 2, 8, 128),
    gains=spec(F32, 8, 1024),
    gg=spec(F32, 8, 1024),
    ggx=spec(F32, 3, 8, 1024),
    ggz=spec(F32, 4, 8, 256),
    ggzr=spec(F32, 3, 8, 256),
    ggy=spec(F32, 2, 8, 128),
    ggyr=spec(F32, 8, 8, 128),
    scores=spec(F32, 16, 128, 512),
    dkvf=spec(F32, 2, 256, 256),
    outst=spec(BF, 4, 32, 256),
    ingst=spec(BF, 4, 32, 256),
    outrv=spec(BF, 2, 64, 256),
    ingrv=spec(BF, 2, 64, 256),
    dmh=spec(BF, 256, 128),
)
LAYER = dict(
    qkst=spec(BF, 2, 32, 256),
    vst=spec(BF, 2, 32, 128),
    gus=spec(BF, 2, 32, 768),
    wds=spec(BF, 96, 256),
    cwo=spec(BF, 32, 256),
    cwd=spec(BF, 96, 256),
    wqk=spec(BF, 4, 8, 32, 256),
    wval=spec(BF, 4, 4, 2, 32, 128),
    wout=spec(BF, 4, 4, 32, 256),
    wgu=spec(BF, 4, 4, 2, 32, 768),
    wdn=spec(BF, 4, 4, 96, 256),
    kv=spec(BF, 4, 2, 256, 256),
    q2=spec(BF, 512, 128),
    prob=spec(BF, 16, 128, 512),
    ot=spec(F32, 128, 256),
    gu=spec(F32, 256, 768),
    hid=spec(BF, 256, 384),
    dkv=spec(BF, 4, 2, 256, 256),
    dkvab=spec(BF, 2, 2, 256, 256),
    dkvc=spec(BF, 256, 256),
    dkvds=spec(BF, 256, 256),
    dkvd=spec(BF, 256, 256),
    dkves=spec(BF, 256, 256),
    dkve=spec(BF, 256, 256),
    gwq=spec(BF, 4, 8, 32, 128),
    gwk=spec(BF, 4, 8, 32, 128),
    gwv=spec(BF, 4, 4, 2, 32, 128),
    gwout=spec(BF, 4, 4, 32, 256),
    gwgu=spec(BF, 4, 4, 2, 32, 768),
    gwdn=spec(BF, 4, 4, 96, 256),
    rzq=spec(BF, 3, 8, 32, 128),
    rzk=spec(BF, 3, 8, 32, 128),
    ryv=spec(BF, 3, 4, 2, 32, 128),
    rzout=spec(BF, 3, 4, 32, 256),
    rygu=spec(BF, 3, 4, 2, 32, 768),
    rzdn=spec(BF, 3, 4, 96, 256),
    sq=spec(BF, 8, 32, 128),
    sk=spec(BF, 8, 32, 128),
    sv=spec(BF, 4, 2, 32, 128),
    sout=spec(BF, 4, 32, 256),
    sgu=spec(BF, 4, 2, 32, 768),
    sdn=spec(BF, 4, 96, 256),
    fq=spec(BF, 8, 32, 128),
    fk=spec(BF, 8, 32, 128),
    fv=spec(BF, 8, 32, 128),
    fgu=spec(BF, 8, 32, 768),
    yout=spec(BF, 4, 32, 256),
    ydn=spec(BF, 4, 96, 256),
    cout=spec(BF, 32, 256),
    cdn=spec(BF, 96, 256),
    fout=spec(BF, 32, 256),
    fdn=spec(BF, 96, 256),
)
SUB = dict(
    a=spec(BF, 8, 32, 1024),
    h=spec(BF, 32, 1024),
    gr=spec(BF, 32, 1024),
    gb=spec(BF, 8, 32, 1024),
)
EXCHANGE = dict(
    pb=spec(BF, 2, 4, 32, 1024),
    sib=spec(BF, 4, 32, 1024),
    xs=spec(BF, 3, 32, 1024),
    xr=spec(BF, 3, 32, 1024),
)
N_SEM = 640
N_LAYERS, N_SUB, N_EXCHANGE = 2, 4, 8


def groups():
    arguments = [(0, 0, COMMON_IN)] + [(1, l, LAYER_IN) for l in range(N_LAYERS)]
    results = [(0, 0, COMMON_OUT)] + [(1, l, LAYER_OUT) for l in range(N_LAYERS)]
    scratch = [(0, 0, COMMON)] + [(1, l, LAYER) for l in range(N_LAYERS)]
    scratch += [(2, i, SUB) for i in range(N_SUB)] + [(3, n, EXCHANGE) for n in range(N_EXCHANGE)]
    return arguments, results, scratch


def named(refs):
    spaces = [[SimpleNamespace() for _ in range(n)] for n in (1, N_LAYERS, N_SUB, N_EXCHANGE)]
    left = list(refs)
    for group in groups():
        for kind, index, specs in group:
            for name in specs:
                setattr(spaces[kind][index], name, left.pop(0))
    return spaces[0][0], spaces[1], spaces[2], spaces[3]


def specs_of(group):
    return [entry for _, _, specs in group for entry in specs.values()]


def nn(a, b):
    return lax.dot_general(a, b, (((1,), (0,)), ((), ())), preferred_element_type=F32)


def nt(a, b):
    return lax.dot_general(a, b, (((1,), (1,)), ((), ())), preferred_element_type=F32)


def tn(a, b):
    return lax.dot_general(a, b, (((0,), (0,)), ((), ())), preferred_element_type=F32)


def normalize(h):
    inverse = lax.rsqrt(jnp.mean(h * h, axis=-1, keepdims=True) + EPS)
    return h * inverse, inverse


def kernel(*refs):
    R, L, S, X = named(refs[:-1])
    sems = refs[-1]
    used = [0]
    pending = []

    def new():
        used[0] += 1
        return sems.at[used[0] - 1]

    x = lax.axis_index("section")
    c = lax.axis_index("ctx")
    z, y, k = lax.div(c, 8), lax.rem(lax.div(c, 2), 4), lax.rem(c, 2)
    t = 2 * x + k
    s = lax.div(y, 2)
    yy = lax.rem(y, 2)
    other = 1 - k

    def plus(v, j):
        return lax.rem(v + j, 4)

    def dev(xd, zd, yd, kd):
        return {"section": xd, "ctx": zd * 8 + yd * 2 + kd}

    def flip(j):
        return k if j % 2 == 0 else other

    sibling = dev(x, z, y, other)

    def put(src, dst, to, rsem):
        copy = pltpu.make_async_remote_copy(
            src_ref=src, dst_ref=dst, send_sem=new(), recv_sem=rsem, device_id=to, device_id_type=MESH
        )
        copy.start()
        pending.append((None, copy))

    def put_or_keep(mine, src, dst, to, rsem):
        copy = pltpu.make_async_remote_copy(
            src_ref=src, dst_ref=dst, send_sem=new(), recv_sem=rsem, device_id=to, device_id_type=MESH
        )

        @pl.when(mine)
        def _():
            pltpu.make_async_copy(src, dst, rsem).start()

        @pl.when(jnp.logical_not(mine))
        def _():
            copy.start()

        pending.append((mine, copy))

    def arrived(ref, sem):
        pltpu.make_async_copy(ref, ref, sem).wait()

    barrier = pltpu.get_barrier_semaphore()

    def greet(d):
        pl.semaphore_signal(barrier, inc=1, device_id=d, device_id_type=MESH)

    count = 0
    for j in range(4):
        for i in range(2):
            if (j, i) != (0, 0):
                greet(dev(plus(x, j), z, y, flip(i)))
                count += 1
            if j:
                greet(dev(x, z, plus(y, j), flip(i)))
                greet(dev(x, plus(z, j), y, flip(i)))
                count += 2
            greet(dev(plus(x, j), 3 - z, 3 - y, flip(i)))
            count += 1
    crossing = jnp.where(x == z, 0, 1)

    @pl.when(x != z)
    def _():
        greet(dev(z, x, y, k))

    lane = lax.broadcasted_iota(I32, (1, 768), 1)
    half = (lane >= 384).astype(I32)
    place = lane - 384 * half
    group = (place >= 96).astype(I32) + (place >= 192).astype(I32) + (place >= 288).astype(I32)
    place = place - 96 * group
    unit = jnp.where(place < 88, 352 * half + 88 * group + place, -1)
    R.pick[...] = (lax.broadcasted_iota(I32, (704, 768), 0) == unit).astype(F32).astype(BF)
    stacked = jnp.concatenate([w[...] for l in range(2) for w in (L[l].wg, L[l].wu)], axis=0)
    stacked = nn(stacked, R.pick[...]).astype(BF)
    for l in range(2):
        for i in range(2):
            L[l].qkst[i, :, 0:128] = L[l].wq[:, 128 * i : 128 * i + 128]
            L[l].qkst[i, :, 128:256] = L[l].wk[:, 128 * i : 128 * i + 128]
            L[l].vst[i] = L[l].wv[:, 128 * i : 128 * i + 128]
            for n in range(2):
                rows = stacked[64 * l + 32 * n : 64 * l + 32 * n + 32, 384 * i : 384 * i + 384]
                L[l].gus[i, :, 384 * n : 384 * n + 384] = rows
        L[l].wds[0:88, :] = L[l].wd[...]
        L[l].wds[88:96, :] = jnp.zeros((8, 256), BF)
    column = lax.broadcasted_iota(I32, (32, 128), 1) - 32 * lax.rem(c, 4)
    spot = (lax.broadcasted_iota(I32, (32, 128), 0) == column).astype(F32).astype(BF)
    piece = nn(jnp.broadcast_to(R.gains_in[...].astype(F32), (8, 32)).astype(BF), spot)
    R.gst[...] = jnp.where(lax.broadcasted_iota(I32, (8, 128), 0) == x, piece, 0.0)
    R.gg[...] = jnp.zeros((8, 1024), F32)
    pl.semaphore_wait(barrier, count + crossing)

    W = [SimpleNamespace(), SimpleNamespace()]
    G = [SimpleNamespace(), SimpleNamespace()]
    partner = dev(x, z, y + 1 - 2 * yy, k)
    mate = 1 - yy
    slot_m = 2 * yy + k

    def keep(src, dst, sem):
        pltpu.make_async_copy(src, dst, sem).start()

    def to_z(src, dst, js=(1, 3, 2)):
        sem = new()
        for j in js:
            put(src, dst, dev(x, plus(z, j), y, k), sem)
        return sem

    def to_y(src, dst, js=(1, 3, 2)):
        sem = new()
        for j in js:
            put(src, dst, dev(x, z, plus(y, j), k), sem)
        return sem

    def qk_first(l):
        src, dst = L[l].qkst, L[l].wqk.at[z, 2 * y + k]
        sem = W[l].qk = new()
        keep(src.at[k], dst, sem)
        for j in (2, 6, 4, 3, 7, 5, 1):
            put(src.at[flip(j)], dst, dev(x, z, plus(y, j // 2), flip(j)), sem)

    def qk_second(l):
        w = L[l].wqk
        arrived(w.at[z], W[l].qk)
        W[l].qk = to_z(w.at[z], w.at[z])

    def z_first(src, w):
        sem, dst = new(), w.at[z, y, k]
        keep(src.at[k], dst, sem)
        for j in (2, 6, 4, 3, 7, 5, 1):
            put(src.at[flip(j)], dst, dev(x, plus(z, j // 2), y, flip(j)), sem)
        return sem

    def v_second(l):
        w = L[l].wval
        arrived(w.at[:, y], W[l].v)
        W[l].v = to_y(w.at[:, y], w.at[:, y])

    def gate_second(l):
        arrived(L[l].wgu.at[:, y], W[l].gu)
        w = L[l].wgu.at[:, y, :, :, 0:384]
        W[l].gate = to_y(w, w)

    def up_second(l):
        w = L[l].wgu.at[:, y, :, :, 384:768]
        W[l].up = to_y(w, w)

    def cross_first(src, dst):
        sem = new()
        put_or_keep(x == z, src, dst, dev(z, x, y, k), sem)
        return sem

    def cross_second(src, w, sem):
        arrived(src, sem)
        sem, dst = new(), w.at[z, slot_m]
        put_or_keep(s == k, src, dst, dev(x, z, y, s), sem)
        for j in (1, 3, 2):
            put(src, dst, dev(x, z, plus(y, j), s), sem)
        return sem

    def cross_third(w, sem):
        arrived(w.at[z], sem)
        return to_z(w.at[z], w.at[z])

    def rs_start(n, part):
        pb, sib = X[n].pb, X[n].sib
        for i in range(8):
            pb[i % 2, i // 2] = part[32 * i : 32 * i + 32].astype(BF)
        sem = [new() for _ in range(4)]
        for j in (1, 3, 2, 0):
            xd = plus(x, j)
            put(pb.at[other, xd], sib.at[xd], sibling, sem[j])
        return sem

    def rs_mid(n, sem):
        pb, sib, xs, xr = X[n].pb, X[n].sib, X[n].xs, X[n].xr
        out = []
        for j in (1, 3, 2):
            xd = plus(x, j)
            arrived(sib.at[xd], sem[j])
            xs[j - 1] = (pb[k, xd].astype(F32) + sib[xd].astype(F32)).astype(BF)
            out.append(new())
            put(xs.at[j - 1], xr.at[j - 1], dev(xd, z, y, k), out[-1])
        return sem[0], out

    def rs_end(n, sems_):
        pb, sib, xr = X[n].pb, X[n].sib, X[n].xr
        own, out = sems_
        arrived(sib.at[x], own)
        total = pb[k, x].astype(F32) + sib[x].astype(F32)
        for j, sem in zip((1, 3, 2), out):
            arrived(xr.at[j - 1], sem)
            total += xr[j - 1].astype(F32)
        return total

    def gather(buf, block):
        buf[t] = block
        rx = [new() for _ in range(4)]
        rk = [new() for _ in range(4)]
        for j in (1, 3, 2):
            put(buf.at[t], buf.at[t], dev(plus(x, j), z, y, k), rx[j])
        put(buf.at[t], buf.at[t], sibling, rk[0])
        for j in (1, 3, 2):
            slot = buf.at[2 * plus(x, 4 - j) + k]
            arrived(slot, rx[j])
            put(slot, slot, sibling, rk[j])
        for j in range(4):
            arrived(buf.at[0], rk[j])

    def to_owners(rows, stage, landing):
        for i in range(4):
            stage[i] = rows[:, 256 * i : 256 * i + 256]
        near = x < 2
        zd, yd = jnp.where(near, z, 3 - z), jnp.where(near, y, 3 - y)
        kd = lax.rem(x, 2)
        sem = new()
        dst = landing.at[s, pl.ds(pl.multiple_of(32 * k, 32), 32)]
        put_or_keep(near & (kd == k), stage.at[x], dst, dev(x, zd, yd, kd), sem)
        for j in range(1, 4):
            xd = plus(x, j)
            put(stage.at[xd], dst, dev(xd, zd, yd, kd), sem)
        return sem

    def spread_tokens(src, dst):
        near, far = pl.ds(2 * k, 2), pl.ds(4 + 2 * k, 2)
        close, mirrored = new(), new()
        put(src.at[1 - s], dst.at[far], dev(x, 3 - z, 3 - y, k), mirrored)
        put(src.at[s], dst.at[near], sibling, close)
        dst[near] = src[s]
        return close, mirrored

    def spread_rest(dst, sems_):
        close, mirrored = sems_
        far = pl.ds(4 + 2 * k, 2)
        arrived(dst.at[far], mirrored)
        put(dst.at[far], dst.at[far], sibling, close)
        arrived(dst.at[0:4], close)

    lane = lax.rem(lax.broadcasted_iota(I32, (1, 512), 1), 256)
    own_block = 4 * z + y
    query_pos = jnp.where(lane < 128, 128 * own_block + lane, 128 * (15 - own_block) + lane - 128)
    ids = R.seg[s]

    def tokens_to(n):
        return jnp.sum(jnp.where(ids <= n, 1.0, 0.0), axis=1, keepdims=True).astype(I32)

    first, second = tokens_to(0), tokens_to(1)
    query_start = jnp.where(query_pos < first, 0, jnp.where(query_pos < second, first, second))
    head_lane = lax.broadcasted_iota(I32, (256, 128), 1) < 64

    def two_heads(v):
        zero = jnp.zeros_like(v)
        return jnp.concatenate([jnp.where(head_lane, v, zero), jnp.where(head_lane, zero, v)], axis=0)

    def own_heads(vt):
        return jnp.concatenate([vt[0:64, 0:256], vt[64:128, 256:512]], axis=0)

    def gain_row(i):
        return R.gains[i : i + 1, :]

    def full(ref):
        return ref[...].reshape(256, 1024)

    def keys_of(l, zz):
        return L[l].kv[zz, :, :, 0:128].reshape(512, 128)

    def values_of(l, zz):
        return L[l].kv[zz, :, :, 128:256].reshape(512, 128)

    def attention_forward(l, hook):
        w = L[l].wqk
        arrived(w.at[0:3], W[l].qk)
        a = full(S[2 * l].a)
        qk = nn(a, w[...].reshape(1024, 256))
        w = L[l].wval
        arrived(w.at[0:3], W[l].v)
        u = nn(a, w[...].reshape(1024, 128))
        q = (qk[:, 0:128].astype(BF) * 0.125).astype(BF)
        keys = qk[:, 128:256].astype(BF)
        if l == 0:
            values = u.astype(BF)
        else:
            values = (0.5 * u + 0.5 * L[0].kv[z, yy, :, 128:256].astype(F32)).astype(BF)
        kv = L[l].kv
        kv[z, yy, :, 0:128] = keys
        kv[z, yy, :, 128:256] = values
        q2 = two_heads(q)
        L[l].q2[...] = q2
        own, near = kv.at[z, yy], kv.at[z, mate]
        direct, relayed, from_mate = [new() for _ in range(4)], [new() for _ in range(4)], new()
        for j in (1, 3):
            put(own, own, dev(x, plus(z, j), y, k), direct[j])
        put(own, own, partner, from_mate)
        put(own, own, dev(x, plus(z, 2), y, k), direct[2])
        arrived(near, from_mate)
        for j in (1, 3):
            put(near, near, dev(x, plus(z, j), y, k), relayed[j])
        scores = R.scores
        top = jnp.full((1, 512), MASKED, F32)
        for j in (0, 3, 1, 2):
            zz = plus(z, j)
            if j % 2:
                arrived(kv.at[zz, yy], direct[4 - j])
                arrived(kv.at[zz, mate], relayed[4 - j])
            elif j:
                arrived(kv.at[zz, mate], relayed[2])
            scores[4 * j : 4 * j + 4] = nt(keys_of(l, zz), L[l].q2[...]).reshape(4, 128, 512)

            def mask(i, top, j=j, zz=zz):
                block = 4 * zz + 2 * s + lax.div(i, 2)
                base = 128 * (block + lax.rem(i, 2) * (15 - 2 * block))
                row = lax.broadcasted_iota(I32, (128, 512), 0)
                seen = (row >= query_start - base) & (row <= query_pos - base)
                v = jnp.where(seen, scores[4 * j + i], MASKED)
                scores[4 * j + i] = v
                return jnp.maximum(top, jnp.max(v, axis=0, keepdims=True))

            top = lax.fori_loop(0, 4, mask, top)
            if j == 0:
                opposite = kv.at[plus(z, 2), yy]
                arrived(opposite, direct[2])
                put(opposite, opposite, partner, relayed[2])
        hook()

        def expo(i, total):
            v = jnp.exp(scores[i] - top)
            scores[i] = v
            return total + jnp.sum(v, axis=0, keepdims=True)

        total = lax.fori_loop(0, 16, expo, jnp.zeros((1, 512), F32))
        share = 1.0 / total
        prob = L[l].prob

        def norm(i, carry):
            prob[i] = (scores[i] * share).astype(BF)
            return carry

        lax.fori_loop(0, 16, norm, 0)
        ot = jnp.zeros((128, 512), F32)
        for j in range(4):
            ot += tn(values_of(l, plus(z, j)), prob[4 * j : 4 * j + 4].reshape(512, 512))
        ot = own_heads(ot)
        L[l].ot[...] = ot
        o = jnp.transpose(ot).astype(BF)
        arrived(L[l].wout.at[0:3], W[l].o)
        return jnp.concatenate([nn(o, L[l].wout[i].reshape(128, 256)) for i in range(4)], axis=1)

    def feedforward_forward(l, hook):
        a, w = full(S[2 * l + 1].a), L[l].wgu
        arrived(w.at[0:3, :, :, :, 0:384], W[l].gate)
        gate = nn(a, w[:, :, :, :, 0:384].reshape(1024, 384))
        arrived(w.at[0:3, :, :, :, 384:768], W[l].up)
        up = nn(a, w[:, :, :, :, 384:768].reshape(1024, 384))
        L[l].gu[:, 0:384] = gate
        L[l].gu[:, 384:768] = up
        hidden = (gate * jax.nn.sigmoid(gate) * up).astype(BF)
        L[l].hid[...] = hidden
        hook()
        arrived(L[l].wdn.at[0:3], W[l].d)
        return jnp.concatenate([nn(hidden, L[l].wdn[i].reshape(384, 256)) for i in range(4)], axis=1)

    def next_rows(i, part, hook=None):
        sems_ = rs_mid(i, rs_start(i, part))
        if hook is not None:
            hook()
        total = rs_end(i, sems_)
        rows = (S[i].h[...].astype(F32) + total).astype(BF)
        S[i + 1].h[...] = rows
        normed, _ = normalize(rows.astype(F32))
        gather(S[i + 1].a, (normed * gain_row(i + 1)).astype(BF))

    def norm_backward(i, da):
        normed, inverse = normalize(S[i].h[...].astype(F32))
        R.gg[i : i + 1, :] = jnp.sum(da * normed, axis=0, keepdims=True)
        scaled = da * gain_row(i)
        mixed = scaled - normed * jnp.mean(scaled * normed, axis=-1, keepdims=True)
        return (S[i].gr[...].astype(F32) + inverse * mixed).astype(BF)

    def send_z(g, landing):
        sem = new()
        for j in (1, 3, 2):
            zd = plus(z, j)
            put(g.at[zd], landing.at[j - 1], dev(x, zd, y, k), sem)
        return sem

    def send_y(g, landing):
        sem = new()
        for j in (1, 3, 2):
            yd = plus(y, j)
            put(g.at[:, yd], landing.at[j - 1], dev(x, z, yd, k), sem)
        return sem

    def attention_backward(l, hook1, hook2):
        i0 = 2 * l
        gb = full(S[i0].gb)
        wo = L[l].wout
        dot_ = nt(wo[0].reshape(128, 256), gb[:, 0:256])
        for i in range(1, 4):
            dot_ += nt(wo[i].reshape(128, 256), gb[:, 256 * i : 256 * i + 256])
        dot_ = dot_.astype(BF).astype(F32)
        do2 = two_heads(jnp.transpose(dot_).astype(BF))
        prod = dot_ * L[l].ot[...]
        delta = jnp.concatenate(
            [jnp.sum(prod[0:64], axis=0, keepdims=True), jnp.sum(prod[64:128], axis=0, keepdims=True)], axis=1
        )
        dkv, prob = L[l].dkv, L[l].prob
        dq = jnp.zeros((128, 512), F32)
        ab, c_sem = [new() for _ in range(4)], new()
        for j in (2, 1, 3, 0):
            zz = plus(z, j)
            p = prob[4 * j : 4 * j + 4].reshape(512, 512)
            dp = nt(values_of(l, zz), do2)
            ds = (p.astype(F32) * (dp - delta)).astype(BF)
            dkv[zz, :, :, 0:128] = nn(ds, L[l].q2[...]).astype(BF).reshape(2, 256, 128)
            dkv[zz, :, :, 128:256] = nn(p, do2).astype(BF).reshape(2, 256, 128)
            if j % 2:
                put(dkv.at[zz], L[l].dkvab.at[j // 2], dev(x, zz, y, k), ab[j])
            elif j:
                put(dkv.at[zz, mate], L[l].dkvc, partner, c_sem)
            dq += tn(keys_of(l, zz), ds)
        dq = jnp.transpose(own_heads(dq) * 0.125).astype(BF)
        gw = L[l].gwout
        otb = L[l].ot[...].astype(BF)
        for i in range(4):
            gw[i] = nn(otb, gb[:, 256 * i : 256 * i + 256]).astype(BF).reshape(4, 32, 256)
        at = jnp.transpose(full(S[i0].a))
        L[l].gwq[...] = nn(at, dq).astype(BF).reshape(4, 8, 32, 128)
        arrived(L[l].dkvc, c_sem)
        far = plus(z, 2)
        L[l].dkvds[...] = (dkv[far, yy].astype(F32) + L[l].dkvc[...].astype(F32)).astype(BF)
        d_sem, e_sem = new(), new()
        put(L[l].dkvds, L[l].dkvd, dev(x, far, y, k), d_sem)
        got = L[l].dkvab
        arrived(got.at[0], ab[1])
        arrived(got.at[1], ab[3])
        R.dkvf[...] = dkv[z].astype(F32) + got[0].astype(F32) + got[1].astype(F32)
        L[l].dkves[...] = R.dkvf[mate].astype(BF)
        put(L[l].dkves, L[l].dkve, partner, e_sem)
        G[l].o = send_z(gw, L[l].rzout)
        G[l].q = send_z(L[l].gwq, L[l].rzq)
        arrived(L[l].dkvd, d_sem)
        arrived(L[l].dkve, e_sem)
        tot = R.dkvf[yy] + L[l].dkvd[...].astype(F32) + L[l].dkve[...].astype(F32)
        dk = tot[:, 0:128].astype(BF)
        dvals = tot[:, 128:256]
        if l == 1:
            half = 0.5 * dvals.astype(BF).astype(F32)
            du = half.astype(BF)
            R.dmh[...] = du
        else:
            du = (dvals + R.dmh[...].astype(F32)).astype(BF)
        da = nt(jnp.concatenate([dq, dk], axis=1), L[l].wqk[...].reshape(1024, 256))
        da += nt(du, L[l].wval[...].reshape(1024, 128))
        rs = rs_start(4 + i0, da)
        grads = nn(at, jnp.concatenate([dk, du], axis=1)).astype(BF)
        L[l].gwk[...] = grads[:, 0:128].reshape(4, 8, 32, 128)
        L[l].gwv[...] = grads[:, 128:256].reshape(4, 4, 2, 32, 128)
        rs = rs_mid(4 + i0, rs)
        G[l].k = send_z(L[l].gwk, L[l].rzk)
        G[l].v = send_y(L[l].gwv, L[l].ryv)
        hook1()
        hook2()
        return norm_backward(i0, rs_end(4 + i0, rs))

    def feedforward_backward(l, hook1, hook2):
        i0 = 2 * l + 1
        gb = full(S[i0].gb)
        wd = L[l].wdn
        dhid = nt(gb[:, 0:256], wd[0].reshape(384, 256))
        for i in range(1, 4):
            dhid += nt(gb[:, 256 * i : 256 * i + 256], wd[i].reshape(384, 256))
        gu = L[l].gu[...]
        gate, up = gu[:, 0:384], gu[:, 384:768]
        sig = jax.nn.sigmoid(gate)
        dgate = dhid * up * sig * (1.0 + gate * (1.0 - sig))
        dup = dhid * (gate * sig)
        dgu = jnp.concatenate([dgate.astype(BF), dup.astype(BF)], axis=1)
        rs = rs_start(4 + i0, nt(dgu, L[l].wgu[...].reshape(1024, 768)))
        hook1()
        rs = rs_mid(4 + i0, rs)
        at = jnp.transpose(full(S[i0].a))
        gw = L[l].gwgu
        gw[...] = nn(at, dgu).astype(BF).reshape(4, 4, 2, 32, 768)
        G[l].g = send_y(gw, L[l].rygu)
        ht = jnp.transpose(L[l].hid[...])
        gw = L[l].gwdn
        for i in range(4):
            gw[i] = nn(ht, gb[:, 256 * i : 256 * i + 256]).astype(BF).reshape(4, 96, 256)
        G[l].d = send_z(gw, L[l].rzdn)
        hook2()
        return norm_backward(i0, rs_end(4 + i0, rs))

    def summed(own, got):
        return own.astype(F32) + got[0].astype(F32) + got[1].astype(F32) + got[2].astype(F32)

    def rows_back(st, land):
        sem = new()
        for j in range(4):
            m = plus(slot_m, j)
            to = dev(x, z, 2 * k + lax.div(m, 2), lax.rem(m, 2))
            if j == 0:
                put_or_keep(s == k, st.at[m], land.at[y], to, sem)
            else:
                put(st.at[m], land.at[y], to, sem)
        return sem

    def four(land):
        return land[0].astype(F32) + land[1].astype(F32) + land[2].astype(F32) + land[3].astype(F32)

    def out_second(l):
        arrived(L[l].rzout, G[l].o)
        L[l].sout[...] = summed(L[l].gwout[z], L[l].rzout).astype(BF)
        G[l].o = rows_back(L[l].sout, L[l].yout)

    def out_third(l):
        arrived(L[l].yout, G[l].o)
        L[l].cout[...] = four(L[l].yout).astype(BF)
        G[l].o = cross_first(L[l].cout, L[l].fout)

    def out_end(l):
        arrived(L[l].fout, G[l].o)
        L[l].oo[...] = L[l].fout[...].astype(F32)

    def down_second(l):
        arrived(L[l].rzdn, G[l].d)
        L[l].sdn[...] = summed(L[l].gwdn[z], L[l].rzdn).astype(BF)
        G[l].d = rows_back(L[l].sdn, L[l].ydn)

    def down_third(l):
        arrived(L[l].ydn, G[l].d)
        L[l].cdn[...] = four(L[l].ydn).astype(BF)
        G[l].d = cross_first(L[l].cdn, L[l].fdn)

    def down_end(l):
        arrived(L[l].fdn, G[l].d)
        L[l].od[...] = L[l].fdn[0:88, :].astype(F32)

    def rows_y(g, got, st, land, sem):
        arrived(got, sem)
        st[...] = summed(g[z], got).astype(BF)
        sem = new()
        land[0] = st[2 * y + k]
        for j in (2, 6, 4, 3, 7, 5, 1):
            yd, kd = plus(y, j // 2), flip(j)
            put(st.at[2 * yd + kd], land.at[j], dev(x, z, yd, kd), sem)
        return sem

    def rows_z(g, got, st, land, sem):
        arrived(got, sem)
        for i in range(4):
            own = g[i, y].astype(F32) + got[0, i].astype(F32) + got[1, i].astype(F32) + got[2, i].astype(F32)
            st[i] = own.astype(BF)
        sem = new()
        land[0] = st[z, k]
        for j in (2, 6, 4, 3, 7, 5, 1):
            zd, kd = plus(z, j // 2), flip(j)
            put(st.at[zd, kd], land.at[j], dev(x, zd, y, kd), sem)
        return sem

    def halves(land, sem):
        arrived(land.at[1:8], sem)
        own = land[0].astype(F32) + land[2].astype(F32) + land[4].astype(F32) + land[6].astype(F32)
        far = land[1].astype(F32) + land[3].astype(F32) + land[5].astype(F32) + land[7].astype(F32)
        return jnp.where(k == 0, own, far), jnp.where(k == 0, far, own)

    def q_second(l):
        G[l].q = rows_y(L[l].gwq, L[l].rzq, L[l].sq, L[l].fq, G[l].q)

    def k_second(l):
        G[l].k = rows_y(L[l].gwk, L[l].rzk, L[l].sk, L[l].fk, G[l].k)

    def v_grad_second(l):
        G[l].v = rows_z(L[l].gwv, L[l].ryv, L[l].sv, L[l].fv, G[l].v)

    def gu_grad_second(l):
        G[l].g = rows_z(L[l].gwgu, L[l].rygu, L[l].sgu, L[l].fgu, G[l].g)

    def att_end(l):
        for land, result, sem in ((L[l].fq, L[l].oq, G[l].q), (L[l].fk, L[l].ok, G[l].k), (L[l].fv, L[l].ov, G[l].v)):
            low, high = halves(land, sem)
            result[:, 0:128] = low
            result[:, 128:256] = high

    def gu_end(l):
        low, high = halves(L[l].fgu, G[l].g)
        both = jnp.concatenate(
            [
                jnp.concatenate([low[:, 0:384], high[:, 0:384]], axis=1),
                jnp.concatenate([low[:, 384:768], high[:, 384:768]], axis=1),
            ],
            axis=0,
        )
        main = both.astype(BF)
        rest = (both - main.astype(F32)).astype(BF)
        both = nt(main, R.pick[...]) + nt(rest, R.pick[...])
        L[l].og[...] = both[0:32]
        L[l].ou[...] = both[32:64]

    def nothing():
        pass

    def att_first(l):
        qk_first(l)
        W[l].v = z_first(L[l].vst, L[l].wval)
        W[l].o = cross_first(L[l].wo, L[l].cwo)

    def ff_first(l):
        W[l].gu = z_first(L[l].gus, L[l].wgu)
        W[l].d = cross_first(L[l].wds, L[l].cwd)

    qk_first(0)
    W[0].v = z_first(L[0].vst, L[0].wval)
    in_sems = spread_tokens(R.xin, R.hin)
    gx_sem = new()
    for j in (1, 3, 2):
        put(R.gst, R.gx.at[j - 1], dev(plus(x, j), z, y, k), gx_sem)
    W[0].o = cross_first(L[0].wo, L[0].cwo)
    arrived(R.gx, gx_sem)
    R.g1[...] = R.gst[...] + R.gx[0] + R.gx[1] + R.gx[2]
    gy_sem = new()
    R.gyr[2 * y + k] = R.g1[...]
    for j in range(1, 8):
        put(R.g1, R.gyr.at[2 * y + k], dev(x, z, plus(y, j // 2), flip(j)), gy_sem)
    qk_second(0)
    v_second(0)
    ff_first(0)
    W[0].o = cross_second(L[0].cwo, L[0].wout, W[0].o)
    arrived(R.gyr.at[0:7], gy_sem)
    for i in range(2):
        R.gz[z, i] = R.gyr[4 * i] + R.gyr[4 * i + 1] + R.gyr[4 * i + 2] + R.gyr[4 * i + 3]
    gz_sem = to_z(R.gz.at[z], R.gz.at[z])
    spread_rest(R.hin, in_sems)
    normed, _ = normalize(full(R.hin).astype(F32))
    S[0].h[...] = R.hin[t]
    arrived(R.gz.at[0:3], gz_sem)
    R.gains[...] = jnp.concatenate([R.gz[i // 2, i % 2] for i in range(8)], axis=1)
    S[0].a[...] = (normed * gain_row(0)).astype(BF).reshape(8, 32, 1024)
    W[0].o = cross_third(L[0].wout, W[0].o)
    gate_second(0)
    W[0].d = cross_second(L[0].cwd, L[0].wdn, W[0].d)
    cot_sems = []

    def after_keys_0():
        up_second(0)
        W[0].d = cross_third(L[0].wdn, W[0].d)
        att_first(1)
        ff_first(1)

    def in_ff_0():
        qk_second(1)
        v_second(1)
        W[1].o = cross_second(L[1].cwo, L[1].wout, W[1].o)

    def after_sum_1():
        W[1].o = cross_third(L[1].wout, W[1].o)
        gate_second(1)
        W[1].d = cross_second(L[1].cwd, L[1].wdn, W[1].d)

    def after_keys_1():
        up_second(1)
        W[1].d = cross_third(L[1].wdn, W[1].d)
        cot_sems.append(spread_tokens(R.cot, S[3].gb))

    def nothing():
        pass

    next_rows(0, attention_forward(0, after_keys_0))
    next_rows(1, feedforward_forward(0, in_ff_0), after_sum_1)
    next_rows(2, attention_forward(1, after_keys_1))
    last = rs_mid(3, rs_start(3, feedforward_forward(1, lambda: spread_rest(S[3].gb, cot_sems[0]))))
    S[3].gr[...] = S[3].gb[t]
    out_sem = []

    def finish_outputs():
        rows = (S[3].h[...].astype(F32) + rs_end(3, last)).astype(BF)
        out_sem.append(to_owners(rows, R.outst, R.outrv))

    def hand_back(i, rows):
        S[i].gr[...] = rows
        gather(S[i].gb, rows)

    def ff_grads(l):
        gu_grad_second(l)
        down_second(l)

    def att_grads():
        out_second(1)
        q_second(1)
        k_second(1)
        v_grad_second(1)

    def last_grads():
        out_second(0)
        q_second(0)
        ff_grads(0)

    hand_back(2, feedforward_backward(1, finish_outputs, nothing))
    hand_back(1, attention_backward(1, lambda: ff_grads(1), nothing))
    down_third(1)
    hand_back(0, feedforward_backward(0, att_grads, lambda: gu_end(1)))
    out_third(1)
    rows = attention_backward(0, last_grads, lambda: att_end(1))
    in_grad_sem = to_owners(rows, R.ingst, R.ingrv)
    gg_sem = new()
    for j in (1, 3, 2):
        put(R.gg, R.ggx.at[j - 1], dev(plus(x, j), z, y, k), gg_sem)
    k_second(0)
    v_grad_second(0)
    out_third(0)
    down_third(0)
    arrived(R.ggx, gg_sem)
    gg = R.gg[...] + R.ggx[0] + R.ggx[1] + R.ggx[2]
    for i in range(4):
        R.ggz[i] = gg[:, 256 * i : 256 * i + 256]
    gg_sem = new()
    for j in (1, 3, 2):
        zd = plus(z, j)
        put(R.ggz.at[zd], R.ggzr.at[j - 1], dev(x, zd, y, k), gg_sem)
    out_end(1)
    down_end(1)
    gu_end(0)
    arrived(R.outrv, out_sem[0])
    R.out[...] = R.outrv[...].reshape(2, 1, 64, 256)
    arrived(R.ggzr, gg_sem)
    gg = R.ggz[z] + R.ggzr[0] + R.ggzr[1] + R.ggzr[2]
    R.ggy[0] = gg[:, 0:128]
    R.ggy[1] = gg[:, 128:256]
    gg_sem = new()
    R.ggyr[0] = R.ggy[s]
    for j in range(1, 8):
        yd = plus(y, j // 2)
        put(R.ggy.at[lax.div(yd, 2)], R.ggyr.at[j], dev(x, z, yd, flip(j)), gg_sem)
    arrived(R.ingrv, in_grad_sem)
    R.ing[...] = R.ingrv[...].reshape(2, 1, 64, 256)
    att_end(0)
    out_end(0)
    down_end(0)
    arrived(R.ggyr.at[1:8], gg_sem)
    gg = R.ggyr[0]
    for j in range(1, 8):
        gg = gg + R.ggyr[j]
    gg = jnp.sum(jnp.where(lax.broadcasted_iota(I32, (8, 128), 0) == x, gg, 0.0), axis=0, keepdims=True)
    part = lax.rem(c, 4)
    gain = jnp.zeros((1, 32), F32)
    for i in range(4):
        gain += jnp.where(part == i, gg[:, 32 * i : 32 * i + 32], 0.0)
    R.ogg[...] = gain
    for mine, copy in pending:
        if mine is None:
            copy.wait_send()
        else:

            @pl.when(jnp.logical_not(mine))
            def _(copy=copy):
                copy.wait_send()

    assert used[0] <= N_SEM, used


def call(*args):
    whole = pl.BlockSpec(memory_space=pltpu.VMEM)
    arguments, results, scratch = (specs_of(group) for group in groups())
    return pl.pallas_call(
        kernel,
        out_shape=[jax.ShapeDtypeStruct(shape, dtype) for shape, dtype in results],
        in_specs=[whole] * len(arguments),
        out_specs=[whole] * len(results),
        scratch_shapes=[pltpu.VMEM(shape, dtype) for shape, dtype in scratch]
        + [pltpu.SemaphoreType.DMA((N_SEM,))],
        compiler_params=pltpu.CompilerParams(
            collective_id=0, has_side_effects=True, vmem_limit_bytes=62 * 1024 * 1024
        ),
    )(*args)


def hand_out(*refs):
    n = len(refs) // 2
    copies = [pltpu.make_async_copy(refs[i], refs[n + i], refs[-1].at[i]) for i in range(n)]
    for copy in copies:
        copy.start()
    for copy in copies:
        copy.wait()


def body(inputs, cotangent, segment_ids, gains, *weights):
    first = (inputs.reshape(2, 2, 32, 1024), cotangent.reshape(2, 2, 32, 1024), segment_ids, gains)
    results = call(*first, *weights)
    anywhere = pl.BlockSpec(memory_space=pl.ANY)
    return tuple(
        pl.pallas_call(
            hand_out,
            out_shape=[jax.ShapeDtypeStruct(r.shape, r.dtype) for r in results],
            in_specs=[pl.BlockSpec(memory_space=pltpu.VMEM)] * len(results),
            out_specs=[anywhere] * len(results),
            scratch_shapes=[pltpu.SemaphoreType.DMA((len(results),))],
        )(*results)
    )


def solution(mesh):
    tokens = P(None, None, "ctx", None)
    weight = P("ctx", "section")
    return jax.shard_map(
        body,
        mesh=mesh,
        in_specs=(tokens, tokens, P(), P("section", "ctx")) + (weight,) * 14,
        out_specs=(P(None, None, "ctx", "section"),) * 2 + (P("section", "ctx"),) + (weight,) * 14,
        check_vma=False,
    )
```

time: 296 us -> 224 us (0.76)
  Pallas kernels: 268 us -> 220 us
  local copies, waits for them, and re-layouts: 19.5 us -> 0 us
  other arithmetic: 3.33 us -> 0 us
    pallas_call x1, Pallas kernels: 268 us -> 218 us  [call(): pl.pallas_call(kernel, out_shape=[jax.ShapeDtypeStruct(shape, dtype) for...]
    unnamed x48 -> x0, local copies, waits for them, and re-layouts: 10.5 us -> none
    reshape x20 -> x0, local copies, waits for them, and re-layouts: 4.56 us -> none  [the longest x8 3.59 us: unpacked(): return g.swapaxes(0, 1).reshape(rows, 2, 4, 96)[..., :88].reshape(rows, 704)]
where the time goes in v1:
time: 224 us; the launch traced here: 221 us
  Pallas kernels  220 us (98%)
    pallas_call x1, Pallas kernels, call(): pl.pallas_call(kernel, out_shape=[jax.ShapeDtypeStruct(shape, dtype) for...  218 us

profile of v1, /device:TPU:4, one launch (start us, length us, event | category | flops | bytes accessed | tf_op | source)
XLA Modules:
  0.0 221.0 jit_solution(16941123752471155744)
XLA Ops:
  0.7 217.7 %shard_map.305 = (bf16[2,1,64,256]{3,2,1,0:T(8,128)(2,1)}, bf16[2,1,64,256]{3,2,1,0:T(8,128)(2,1)}, f32[1,32]{1,0:T(1,128)}, f32[32,256]{1,0:T(8,128)}, f32[32,2...) custom-call(bf16[2,2,32,1024]{3,2,1,0:T(8,128)(2,1)} %bitcast.2, ...), custom_call_target="tpu_custom_call" | custom-call | tf_op jit(solution)/shard_map/pallas_call | solution.py:948
  218.4 2.4 %shard_map.306 = (bf16[2,1,64,256]{3,2,1,0:T(8,128)(2,1)}, bf16[2,1,64,256]{3,2,1,0:T(8,128)(2,1)}, f32[1,32]{1,0:T(1,128)}, f32[32,256]{1,0:T(8,128)}, f32[32,2...) custom-call(bf16[2,1,64,256]{3,2,1,0:T(8,128)(2,1)} %get-tuple-eleme, ...), custom_call_target="tpu_custom_call" | custom-call | tf_op jit(solution)/shard_map/pallas_call | solution.py:975

commit v2 on v1

--- a/solution.py
+++ b/solution.py
@@ -29,7 +29,7 @@
     wd=spec(BF, 88, 256),
 )
 COMMON_IN = dict(
-    xin=spec(BF, 2, 2, 32, 1024), cot=spec(BF, 2, 2, 32, 1024), seg=spec(I32, 2, 1, 2048), gains_in=spec(BF, 1, 32)
+    xin=spec(BF, 2, 4, 16, 1024), cot=spec(BF, 2, 4, 16, 1024), seg=spec(I32, 2, 1, 2048), gains_in=spec(BF, 1, 32)
 )
 LAYER_OUT = dict(
     oq=spec(F32, 32, 256),
@@ -42,7 +42,7 @@
 )
 COMMON_OUT = dict(out=spec(BF, 2, 1, 64, 256), ing=spec(BF, 2, 1, 64, 256), ogg=spec(F32, 1, 32))
 COMMON = dict(
-    hin=spec(BF, 8, 32, 1024),
+    hin=spec(BF, 2, 8, 16, 1024),
     pick=spec(BF, 704, 768),
     gst=spec(F32, 8, 128),
     gx=spec(F32, 3, 8, 128),
@@ -58,11 +58,14 @@
     ggyr=spec(F32, 8, 8, 128),
     scores=spec(F32, 16, 128, 512),
     dkvf=spec(F32, 2, 256, 256),
-    outst=spec(BF, 4, 32, 256),
-    ingst=spec(BF, 4, 32, 256),
+    outst=spec(BF, 2, 4, 16, 256),
+    ingst=spec(BF, 2, 4, 16, 256),
     outrv=spec(BF, 2, 64, 256),
     ingrv=spec(BF, 2, 64, 256),
     dmh=spec(BF, 256, 128),
+    ds=spec(BF, 4, 512, 512),
+    do2=spec(BF, 512, 128),
+    dgu=spec(BF, 2, 128, 768),
 )
 LAYER = dict(
     qkst=spec(BF, 2, 32, 256),
@@ -76,7 +79,7 @@
     wout=spec(BF, 4, 4, 32, 256),
     wgu=spec(BF, 4, 4, 2, 32, 768),
     wdn=spec(BF, 4, 4, 96, 256),
-    kv=spec(BF, 4, 2, 256, 256),
+    kv=spec(BF, 4, 2, 2, 128, 256),
     q2=spec(BF, 512, 128),
     prob=spec(BF, 16, 128, 512),
     ot=spec(F32, 128, 256),
@@ -99,8 +102,11 @@
     rzk=spec(BF, 3, 8, 32, 128),
     ryv=spec(BF, 3, 4, 2, 32, 128),
     rzout=spec(BF, 3, 4, 32, 256),
-    rygu=spec(BF, 3, 4, 2, 32, 768),
-    rzdn=spec(BF, 3, 4, 96, 256),
+    hygu=spec(BF, 2, 2, 2, 32, 768),
+    bygu=spec(BF, 2, 4, 2, 32, 768),
+    hzdn=spec(BF, 2, 2, 96, 256),
+    bzdn=spec(BF, 2, 4, 96, 256),
+    share=spec(F32, 8, 512),
     sq=spec(BF, 8, 32, 128),
     sk=spec(BF, 8, 32, 128),
     sv=spec(BF, 4, 2, 32, 128),
@@ -119,18 +125,18 @@
     fdn=spec(BF, 96, 256),
 )
 SUB = dict(
-    a=spec(BF, 8, 32, 1024),
-    h=spec(BF, 32, 1024),
-    gr=spec(BF, 32, 1024),
-    gb=spec(BF, 8, 32, 1024),
+    a=spec(BF, 2, 8, 16, 1024),
+    h=spec(BF, 2, 16, 1024),
+    gr=spec(BF, 2, 16, 1024),
+    gb=spec(BF, 2, 8, 16, 1024),
 )
 EXCHANGE = dict(
-    pb=spec(BF, 2, 4, 32, 1024),
-    sib=spec(BF, 4, 32, 1024),
-    xs=spec(BF, 3, 32, 1024),
-    xr=spec(BF, 3, 32, 1024),
+    pb=spec(BF, 2, 2, 4, 16, 1024),
+    sib=spec(BF, 2, 4, 16, 1024),
+    xs=spec(BF, 2, 3, 16, 1024),
+    xr=spec(BF, 2, 3, 16, 1024),
 )
-N_SEM = 640
+N_SEM = 960
 N_LAYERS, N_SUB, N_EXCHANGE = 2, 4, 8
 
 
@@ -250,30 +256,37 @@
     def _():
         greet(dev(z, x, y, k))
 
-    lane = lax.broadcasted_iota(I32, (1, 768), 1)
-    half = (lane >= 384).astype(I32)
-    place = lane - 384 * half
-    group = (place >= 96).astype(I32) + (place >= 192).astype(I32) + (place >= 288).astype(I32)
-    place = place - 96 * group
-    unit = jnp.where(place < 88, 352 * half + 88 * group + place, -1)
-    R.pick[...] = (lax.broadcasted_iota(I32, (704, 768), 0) == unit).astype(F32).astype(BF)
-    stacked = jnp.concatenate([w[...] for l in range(2) for w in (L[l].wg, L[l].wu)], axis=0)
-    stacked = nn(stacked, R.pick[...]).astype(BF)
-    for l in range(2):
+    def pack_att(l):
         for i in range(2):
             L[l].qkst[i, :, 0:128] = L[l].wq[:, 128 * i : 128 * i + 128]
             L[l].qkst[i, :, 128:256] = L[l].wk[:, 128 * i : 128 * i + 128]
             L[l].vst[i] = L[l].wv[:, 128 * i : 128 * i + 128]
-            for n in range(2):
-                rows = stacked[64 * l + 32 * n : 64 * l + 32 * n + 32, 384 * i : 384 * i + 384]
-                L[l].gus[i, :, 384 * n : 384 * n + 384] = rows
-        L[l].wds[0:88, :] = L[l].wd[...]
-        L[l].wds[88:96, :] = jnp.zeros((8, 256), BF)
+
+    def pack_rest():
+        lane = lax.broadcasted_iota(I32, (1, 768), 1)
+        half = (lane >= 384).astype(I32)
+        place = lane - 384 * half
+        group = (place >= 96).astype(I32) + (place >= 192).astype(I32) + (place >= 288).astype(I32)
+        place = place - 96 * group
+        unit = jnp.where(place < 88, 352 * half + 88 * group + place, -1)
+        R.pick[...] = (lax.broadcasted_iota(I32, (704, 768), 0) == unit).astype(F32).astype(BF)
+        stacked = jnp.concatenate([w[...] for l in range(2) for w in (L[l].wg, L[l].wu)], axis=0)
+        stacked = nn(stacked, R.pick[...]).astype(BF)
+        for l in range(2):
+            for i in range(2):
+                for n in range(2):
+                    rows = stacked[64 * l + 32 * n : 64 * l + 32 * n + 32, 384 * i : 384 * i + 384]
+                    L[l].gus[i, :, 384 * n : 384 * n + 384] = rows
+            L[l].wds[0:88, :] = L[l].wd[...]
+            L[l].wds[88:96, :] = jnp.zeros((8, 256), BF)
+        pack_att(1)
+        R.gg[...] = jnp.zeros((8, 1024), F32)
+
+    pack_att(0)
     column = lax.broadcasted_iota(I32, (32, 128), 1) - 32 * lax.rem(c, 4)
     spot = (lax.broadcasted_iota(I32, (32, 128), 0) == column).astype(F32).astype(BF)
     piece = nn(jnp.broadcast_to(R.gains_in[...].astype(F32), (8, 32)).astype(BF), spot)
     R.gst[...] = jnp.where(lax.broadcasted_iota(I32, (8, 128), 0) == x, piece, 0.0)
-    R.gg[...] = jnp.zeros((8, 1024), F32)
     pl.semaphore_wait(barrier, count + crossing)
 
     W = [SimpleNamespace(), SimpleNamespace()]
@@ -321,14 +334,45 @@
         arrived(w.at[:, y], W[l].v)
         W[l].v = to_y(w.at[:, y], w.at[:, y])
 
-    def gate_second(l):
+    def at_y(j):
+        return dev(x, z, plus(y, j), k)
+
+    def at_z(j):
+        return dev(x, plus(z, j), y, k)
+
+    def ring_start(block, v, at):
+        sems_ = [new() for _ in range(4)]
+        put(block(v), block(v), at(1), sems_[0])
+        put(block(v), block(v), at(3), sems_[1])
+        return block, v, at, sems_
+
+    def ring_relay(state):
+        block, v, at, sems_ = state
+        before, after = plus(v, 3), plus(v, 1)
+        arrived(block(before), sems_[0])
+        put(block(before, 0), block(before, 0), at(1), sems_[2])
+        arrived(block(after), sems_[1])
+        put(block(after, 1), block(after, 1), at(3), sems_[3])
+
+    def ring_end(state):
+        block, v, at, sems_ = state
+        far = plus(v, 2)
+        arrived(block(far, 0), sems_[2])
+        arrived(block(far, 1), sems_[3])
+
+    def halved(h):
+        return slice(None) if h is None else slice(2 * h, 2 * h + 2)
+
+    def gate_start(l):
         arrived(L[l].wgu.at[:, y], W[l].gu)
-        w = L[l].wgu.at[:, y, :, :, 0:384]
-        W[l].gate = to_y(w, w)
-
-    def up_second(l):
-        w = L[l].wgu.at[:, y, :, :, 384:768]
-        W[l].up = to_y(w, w)
+        W[l].gate = ring_start(lambda v, h=None: L[l].wgu.at[halved(h), v, :, :, 0:384], y, at_y)
+
+    def up_start(l):
+        W[l].up = ring_start(lambda v, h=None: L[l].wgu.at[halved(h), v, :, :, 384:768], y, at_y)
+
+    def down_start(l):
+        arrived(L[l].wdn.at[z], W[l].d)
+        W[l].d = ring_start(lambda v, h=None: L[l].wdn.at[v, halved(h)], z, at_z)
 
     def cross_first(src, dst):
         sem = new()
@@ -347,83 +391,115 @@
         arrived(w.at[z], sem)
         return to_z(w.at[z], w.at[z])
 
-    def rs_start(n, part):
+    streams = (0, 1)
+    sums = {}
+
+    def rs_start(n, i, part):
         pb, sib = X[n].pb, X[n].sib
-        for i in range(8):
-            pb[i % 2, i // 2] = part[32 * i : 32 * i + 32].astype(BF)
-        sem = [new() for _ in range(4)]
+        for r in range(8):
+            pb[i, r % 2, r // 2] = part[16 * r : 16 * r + 16].astype(BF)
+        sem = sums[n, i] = [new() for _ in range(4)]
         for j in (1, 3, 2, 0):
             xd = plus(x, j)
-            put(pb.at[other, xd], sib.at[xd], sibling, sem[j])
-        return sem
-
-    def rs_mid(n, sem):
+            put(pb.at[i, other, xd], sib.at[i, xd], sibling, sem[j])
+
+    def rs_mid(n, i):
         pb, sib, xs, xr = X[n].pb, X[n].sib, X[n].xs, X[n].xr
-        out = []
+        sem, out = sums[n, i], []
         for j in (1, 3, 2):
             xd = plus(x, j)
-            arrived(sib.at[xd], sem[j])
-            xs[j - 1] = (pb[k, xd].astype(F32) + sib[xd].astype(F32)).astype(BF)
+            arrived(sib.at[i, xd], sem[j])
+            xs[i, j - 1] = (pb[i, k, xd].astype(F32) + sib[i, xd].astype(F32)).astype(BF)
             out.append(new())
-            put(xs.at[j - 1], xr.at[j - 1], dev(xd, z, y, k), out[-1])
-        return sem[0], out
-
-    def rs_end(n, sems_):
+            put(xs.at[i, j - 1], xr.at[i, j - 1], dev(xd, z, y, k), out[-1])
+        sums[n, i] = sem[0], out
+
+    def rs_end(n, i):
         pb, sib, xr = X[n].pb, X[n].sib, X[n].xr
-        own, out = sems_
-        arrived(sib.at[x], own)
-        total = pb[k, x].astype(F32) + sib[x].astype(F32)
+        own, out = sums[n, i]
+        arrived(sib.at[i, x], own)
+        total = pb[i, k, x].astype(F32) + sib[i, x].astype(F32)
         for j, sem in zip((1, 3, 2), out):
-            arrived(xr.at[j - 1], sem)
-            total += xr[j - 1].astype(F32)
+            arrived(xr.at[i, j - 1], sem)
+            total += xr[i, j - 1].astype(F32)
         return total
 
-    def gather(buf, block):
-        buf[t] = block
+    def gather_start(buf, i, block):
+        buf[i, t] = block
+        mine = buf.at[i, t]
         rx = [new() for _ in range(4)]
         rk = [new() for _ in range(4)]
         for j in (1, 3, 2):
-            put(buf.at[t], buf.at[t], dev(plus(x, j), z, y, k), rx[j])
-        put(buf.at[t], buf.at[t], sibling, rk[0])
-        for j in (1, 3, 2):
-            slot = buf.at[2 * plus(x, 4 - j) + k]
-            arrived(slot, rx[j])
-            put(slot, slot, sibling, rk[j])
+            put(mine, mine, dev(plus(x, j), z, y, k), rx[j])
+        put(mine, mine, sibling, rk[0])
+        return buf, i, rx, rk
+
+    def gather_forward(state):
+        if state is not None:
+            buf, i, rx, rk = state
+            for j in (1, 3, 2):
+                slot = buf.at[i, 2 * plus(x, 4 - j) + k]
+                arrived(slot, rx[j])
+                put(slot, slot, sibling, rk[j])
+
+    def gather_finish(state):
+        if state is not None:
+            buf, i, rx, rk = state
+            for j in range(4):
+                arrived(buf.at[i, 0], rk[j])
+
+    def nothing():
+        pass
+
+    def opened(states, n, work, early=nothing):
+        gather_finish(states[0])
+        work(0)
+        gather_forward(states[1])
+        rs_mid(n, 0)
+        early()
+        gather_finish(states[1])
+        work(1)
+        rs_mid(n, 1)
+
+    def closed(rows_of, buf, between):
+        first = gather_start(buf, 0, rows_of(0))
+        second = gather_start(buf, 1, rows_of(1))
+        between()
+        gather_forward(first)
+        return first, second
+
+    def to_owners(i, rows, stage, landing, sem):
+        for r in range(4):
+            stage[i, r] = rows[:, 256 * r : 256 * r + 256]
+        zd, yd = (z, y) if i == 0 else (3 - z, 3 - y)
+        kd = lax.div(x, 2)
+        first_row = pl.multiple_of(16 * (2 * lax.rem(x, 2) + k), 16)
+        dst = landing.at[s, pl.ds(first_row, 16)]
         for j in range(4):
-            arrived(buf.at[0], rk[j])
-
-    def to_owners(rows, stage, landing):
-        for i in range(4):
-            stage[i] = rows[:, 256 * i : 256 * i + 256]
-        near = x < 2
-        zd, yd = jnp.where(near, z, 3 - z), jnp.where(near, y, 3 - y)
-        kd = lax.rem(x, 2)
-        sem = new()
-        dst = landing.at[s, pl.ds(pl.multiple_of(32 * k, 32), 32)]
-        put_or_keep(near & (kd == k), stage.at[x], dst, dev(x, zd, yd, kd), sem)
-        for j in range(1, 4):
             xd = plus(x, j)
-            put(stage.at[xd], dst, dev(xd, zd, yd, kd), sem)
-        return sem
+            if i == 0 and j == 0:
+                put_or_keep(kd == k, stage.at[i, xd], dst, dev(xd, zd, yd, kd), sem)
+            else:
+                put(stage.at[i, xd], dst, dev(xd, zd, yd, kd), sem)
 
     def spread_tokens(src, dst):
-        near, far = pl.ds(2 * k, 2), pl.ds(4 + 2 * k, 2)
+        rows = pl.ds(4 * k, 4)
         close, mirrored = new(), new()
-        put(src.at[1 - s], dst.at[far], dev(x, 3 - z, 3 - y, k), mirrored)
-        put(src.at[s], dst.at[near], sibling, close)
-        dst[near] = src[s]
+        put(src.at[1 - s], dst.at[1, rows], dev(x, 3 - z, 3 - y, k), mirrored)
+        put(src.at[s], dst.at[0, rows], sibling, close)
+        dst[0, rows] = src[s]
         return close, mirrored
 
     def spread_rest(dst, sems_):
         close, mirrored = sems_
-        far = pl.ds(4 + 2 * k, 2)
-        arrived(dst.at[far], mirrored)
-        put(dst.at[far], dst.at[far], sibling, close)
-        arrived(dst.at[0:4], close)
-
-    lane = lax.rem(lax.broadcasted_iota(I32, (1, 512), 1), 256)
+        far = dst.at[1, pl.ds(4 * k, 4)]
+        arrived(far, mirrored)
+        put(far, far, sibling, close)
+        arrived(dst.at[0], close)
+
+    lane = lax.broadcasted_iota(I32, (1, 512), 1)
     own_block = 4 * z + y
-    query_pos = jnp.where(lane < 128, 128 * own_block + lane, 128 * (15 - own_block) + lane - 128)
+    query_pos = 128 * jnp.where(lane < 256, own_block, 15 - own_block) + lax.rem(lane, 128)
     ids = R.seg[s]
 
     def tokens_to(n):
@@ -431,14 +507,14 @@
 
     first, second = tokens_to(0), tokens_to(1)
     query_start = jnp.where(query_pos < first, 0, jnp.where(query_pos < second, first, second))
-    head_lane = lax.broadcasted_iota(I32, (256, 128), 1) < 64
+    head_lane = lax.broadcasted_iota(I32, (128, 128), 1) < 64
 
     def two_heads(v):
         zero = jnp.zeros_like(v)
         return jnp.concatenate([jnp.where(head_lane, v, zero), jnp.where(head_lane, zero, v)], axis=0)
 
     def own_heads(vt):
-        return jnp.concatenate([vt[0:64, 0:256], vt[64:128, 256:512]], axis=0)
+        return jnp.concatenate([vt[0:64, 0:128], vt[64:128, 128:256]], axis=0)
 
     def gain_row(i):
         return R.gains[i : i + 1, :]
@@ -447,48 +523,55 @@
         return ref[...].reshape(256, 1024)
 
     def keys_of(l, zz):
-        return L[l].kv[zz, :, :, 0:128].reshape(512, 128)
+        return L[l].kv[zz, :, :, :, 0:128].reshape(512, 128)
 
     def values_of(l, zz):
-        return L[l].kv[zz, :, :, 128:256].reshape(512, 128)
-
-    def attention_forward(l, hook):
-        w = L[l].wqk
-        arrived(w.at[0:3], W[l].qk)
-        a = full(S[2 * l].a)
-        qk = nn(a, w[...].reshape(1024, 256))
-        w = L[l].wval
-        arrived(w.at[0:3], W[l].v)
-        u = nn(a, w[...].reshape(1024, 128))
-        q = (qk[:, 0:128].astype(BF) * 0.125).astype(BF)
-        keys = qk[:, 128:256].astype(BF)
-        if l == 0:
-            values = u.astype(BF)
-        else:
-            values = (0.5 * u + 0.5 * L[0].kv[z, yy, :, 128:256].astype(F32)).astype(BF)
+        return L[l].kv[zz, :, :, :, 128:256].reshape(512, 128)
+
+    def attention_forward(l, states, hook, late):
         kv = L[l].kv
-        kv[z, yy, :, 0:128] = keys
-        kv[z, yy, :, 128:256] = values
-        q2 = two_heads(q)
-        L[l].q2[...] = q2
-        own, near = kv.at[z, yy], kv.at[z, mate]
-        direct, relayed, from_mate = [new() for _ in range(4)], [new() for _ in range(4)], new()
-        for j in (1, 3):
-            put(own, own, dev(x, plus(z, j), y, k), direct[j])
-        put(own, own, partner, from_mate)
-        put(own, own, dev(x, plus(z, 2), y, k), direct[2])
-        arrived(near, from_mate)
-        for j in (1, 3):
-            put(near, near, dev(x, plus(z, j), y, k), relayed[j])
+        direct, relayed = [[new() for _ in range(4)] for _ in streams], [[new() for _ in range(4)] for _ in streams]
+        from_mate = [new() for _ in streams]
+        for i in streams:
+            if i == 1:
+                gather_forward(states[1])
+            gather_finish(states[i])
+            a = S[2 * l].a[i].reshape(128, 1024)
+            w = L[l].wqk
+            if i == 0:
+                arrived(w.at[0:3], W[l].qk)
+            qk = nn(a, w[...].reshape(1024, 256))
+            w = L[l].wval
+            if i == 0:
+                arrived(w.at[0:3], W[l].v)
+            u = nn(a, w[...].reshape(1024, 128))
+            if l == 0:
+                values = u.astype(BF)
+            else:
+                values = (0.5 * u + 0.5 * L[0].kv[z, yy, i, :, 128:256].astype(F32)).astype(BF)
+            kv[z, yy, i, :, 0:128] = qk[:, 128:256].astype(BF)
+            kv[z, yy, i, :, 128:256] = values
+            own = kv.at[z, yy, i]
+            for j in (1, 3):
+                put(own, own, dev(x, plus(z, j), y, k), direct[i][j])
+            put(own, own, partner, from_mate[i])
+            put(own, own, dev(x, plus(z, 2), y, k), direct[i][2])
+            L[l].q2[256 * i : 256 * i + 256, :] = two_heads((qk[:, 0:128].astype(BF) * 0.125).astype(BF))
+        for i in streams:
+            near = kv.at[z, mate, i]
+            arrived(near, from_mate[i])
+            for j in (1, 3):
+                put(near, near, dev(x, plus(z, j), y, k), relayed[i][j])
         scores = R.scores
         top = jnp.full((1, 512), MASKED, F32)
         for j in (0, 3, 1, 2):
             zz = plus(z, j)
-            if j % 2:
-                arrived(kv.at[zz, yy], direct[4 - j])
-                arrived(kv.at[zz, mate], relayed[4 - j])
-            elif j:
-                arrived(kv.at[zz, mate], relayed[2])
+            for i in streams:
+                if j % 2:
+                    arrived(kv.at[zz, yy, i], direct[i][4 - j])
+                    arrived(kv.at[zz, mate, i], relayed[i][4 - j])
+                elif j:
+                    arrived(kv.at[zz, mate, i], relayed[i][2])
             scores[4 * j : 4 * j + 4] = nt(keys_of(l, zz), L[l].q2[...]).reshape(4, 128, 512)
 
             def mask(i, top, j=j, zz=zz):
@@ -502,64 +585,90 @@
 
             top = lax.fori_loop(0, 4, mask, top)
             if j == 0:
-                opposite = kv.at[plus(z, 2), yy]
-                arrived(opposite, direct[2])
-                put(opposite, opposite, partner, relayed[2])
+                for i in streams:
+                    opposite = kv.at[plus(z, 2), yy, i]
+                    arrived(opposite, direct[i][2])
+                    put(opposite, opposite, partner, relayed[i][2])
         hook()
-
-        def expo(i, total):
-            v = jnp.exp(scores[i] - top)
-            scores[i] = v
-            return total + jnp.sum(v, axis=0, keepdims=True)
-
-        total = lax.fori_loop(0, 16, expo, jnp.zeros((1, 512), F32))
-        share = 1.0 / total
         prob = L[l].prob
-
-        def norm(i, carry):
-            prob[i] = (scores[i] * share).astype(BF)
-            return carry
-
-        lax.fori_loop(0, 16, norm, 0)
-        ot = jnp.zeros((128, 512), F32)
-        for j in range(4):
-            ot += tn(values_of(l, plus(z, j)), prob[4 * j : 4 * j + 4].reshape(512, 512))
-        ot = own_heads(ot)
-        L[l].ot[...] = ot
-        o = jnp.transpose(ot).astype(BF)
-        arrived(L[l].wout.at[0:3], W[l].o)
-        return jnp.concatenate([nn(o, L[l].wout[i].reshape(128, 256)) for i in range(4)], axis=1)
-
-    def feedforward_forward(l, hook):
-        a, w = full(S[2 * l + 1].a), L[l].wgu
-        arrived(w.at[0:3, :, :, :, 0:384], W[l].gate)
-        gate = nn(a, w[:, :, :, :, 0:384].reshape(1024, 384))
-        arrived(w.at[0:3, :, :, :, 384:768], W[l].up)
-        up = nn(a, w[:, :, :, :, 384:768].reshape(1024, 384))
-        L[l].gu[:, 0:384] = gate
-        L[l].gu[:, 384:768] = up
-        hidden = (gate * jax.nn.sigmoid(gate) * up).astype(BF)
-        L[l].hid[...] = hidden
+        for i in streams:
+            lanes = slice(256 * i, 256 * i + 256)
+            high = top[:, lanes]
+
+            def expo(r, total):
+                v = jnp.exp(scores[r, :, lanes] - high)
+                prob[r, :, lanes] = v.astype(BF)
+                return total + jnp.sum(v, axis=0, keepdims=True)
+
+            share = 1.0 / lax.fori_loop(0, 16, expo, jnp.zeros((1, 256), F32))
+            L[l].share[0:1, lanes] = share
+            ot = jnp.zeros((128, 256), F32)
+            for j in range(4):
+                ot += tn(values_of(l, plus(z, j)), prob[4 * j : 4 * j + 4, :, lanes].reshape(512, 256))
+            ot = ot * share
+            ot = own_heads(ot)
+            L[l].ot[:, 128 * i : 128 * i + 128] = ot
+            o = jnp.transpose(ot).astype(BF)
+            if i == 0:
+                arrived(L[l].wout.at[0:3], W[l].o)
+            part = jnp.concatenate([nn(o, L[l].wout[r].reshape(128, 256)) for r in range(4)], axis=1)
+            rs_start(2 * l, i, part)
+        for i in streams:
+            rs_mid(2 * l, i)
+        late()
+
+    def feedforward_forward(l, states, early, hook):
+        w = L[l].wgu
+
+        def work(i):
+            a = S[2 * l + 1].a[i].reshape(128, 1024)
+            if i == 0:
+                ring_end(W[l].gate)
+            gate = nn(a, w[:, :, :, :, 0:384].reshape(1024, 384))
+            if i == 0:
+                ring_end(W[l].up)
+            up = nn(a, w[:, :, :, :, 384:768].reshape(1024, 384))
+            rows = slice(128 * i, 128 * i + 128)
+            L[l].gu[rows, 0:384] = gate
+            L[l].gu[rows, 384:768] = up
+            hidden = (gate * jax.nn.sigmoid(gate) * up).astype(BF)
+            L[l].hid[rows, :] = hidden
+            if i == 0:
+                ring_end(W[l].d)
+            part = jnp.concatenate([nn(hidden, L[l].wdn[r].reshape(384, 256)) for r in range(4)], axis=1)
+            rs_start(2 * l + 1, i, part)
+
+        opened(states, 2 * l + 1, work, early)
         hook()
-        arrived(L[l].wdn.at[0:3], W[l].d)
-        return jnp.concatenate([nn(hidden, L[l].wdn[i].reshape(384, 256)) for i in range(4)], axis=1)
-
-    def next_rows(i, part, hook=None):
-        sems_ = rs_mid(i, rs_start(i, part))
-        if hook is not None:
-            hook()
-        total = rs_end(i, sems_)
-        rows = (S[i].h[...].astype(F32) + total).astype(BF)
-        S[i + 1].h[...] = rows
-        normed, _ = normalize(rows.astype(F32))
-        gather(S[i + 1].a, (normed * gain_row(i + 1)).astype(BF))
-
-    def norm_backward(i, da):
-        normed, inverse = normalize(S[i].h[...].astype(F32))
-        R.gg[i : i + 1, :] = jnp.sum(da * normed, axis=0, keepdims=True)
-        scaled = da * gain_row(i)
+
+    def next_rows(n, between=nothing):
+        def rows_of(i):
+            rows = (S[n].h[i].astype(F32) + rs_end(n, i)).astype(BF)
+            S[n + 1].h[i] = rows
+            normed, _ = normalize(rows.astype(F32))
+            return (normed * gain_row(n + 1)).astype(BF)
+
+        return closed(rows_of, S[n + 1].a, between)
+
+    def norm_backward(n, i):
+        da = rs_end(4 + n, i)
+        normed, inverse = normalize(S[n].h[i].astype(F32))
+        gain_part = jnp.sum(da * normed, axis=0, keepdims=True)
+        if i == 0:
+            R.gg[n : n + 1, :] = gain_part
+        else:
+            R.gg[n : n + 1, :] += gain_part
+        scaled = da * gain_row(n)
         mixed = scaled - normed * jnp.mean(scaled * normed, axis=-1, keepdims=True)
-        return (S[i].gr[...].astype(F32) + inverse * mixed).astype(BF)
+        return (S[n].gr[i].astype(F32) + inverse * mixed).astype(BF)
+
+    def hand_back(n, between=nothing):
+        def rows_of(i):
+            rows = norm_backward(n, i)
+            S[n - 1].gr[i] = rows
+            return rows
+
+        return closed(rows_of, S[n - 1].gb, between)
 
     def send_z(g, landing):
         sem = new()
@@ -575,40 +684,54 @@
             put(g.at[:, yd], landing.at[j - 1], dev(x, z, yd, k), sem)
         return sem
 
-    def attention_backward(l, hook1, hook2):
-        i0 = 2 * l
-        gb = full(S[i0].gb)
-        wo = L[l].wout
-        dot_ = nt(wo[0].reshape(128, 256), gb[:, 0:256])
-        for i in range(1, 4):
-            dot_ += nt(wo[i].reshape(128, 256), gb[:, 256 * i : 256 * i + 256])
-        dot_ = dot_.astype(BF).astype(F32)
-        do2 = two_heads(jnp.transpose(dot_).astype(BF))
-        prod = dot_ * L[l].ot[...]
-        delta = jnp.concatenate(
-            [jnp.sum(prod[0:64], axis=0, keepdims=True), jnp.sum(prod[64:128], axis=0, keepdims=True)], axis=1
-        )
-        dkv, prob = L[l].dkv, L[l].prob
-        dq = jnp.zeros((128, 512), F32)
+    def attention_backward(l, states, hook):
+        n = 2 * l
+        wo, dkv, prob = L[l].wout, L[l].dkv, L[l].prob
         ab, c_sem = [new() for _ in range(4)], new()
-        for j in (2, 1, 3, 0):
-            zz = plus(z, j)
-            p = prob[4 * j : 4 * j + 4].reshape(512, 512)
-            dp = nt(values_of(l, zz), do2)
-            ds = (p.astype(F32) * (dp - delta)).astype(BF)
-            dkv[zz, :, :, 0:128] = nn(ds, L[l].q2[...]).astype(BF).reshape(2, 256, 128)
-            dkv[zz, :, :, 128:256] = nn(p, do2).astype(BF).reshape(2, 256, 128)
-            if j % 2:
-                put(dkv.at[zz], L[l].dkvab.at[j // 2], dev(x, zz, y, k), ab[j])
-            elif j:
-                put(dkv.at[zz, mate], L[l].dkvc, partner, c_sem)
-            dq += tn(keys_of(l, zz), ds)
-        dq = jnp.transpose(own_heads(dq) * 0.125).astype(BF)
+        dq = []
+        for i in streams:
+            if i == 1:
+                gather_forward(states[1])
+            gather_finish(states[i])
+            gb = S[n].gb[i].reshape(128, 1024)
+            dot_ = nt(wo[0].reshape(128, 256), gb[:, 0:256])
+            for r in range(1, 4):
+                dot_ += nt(wo[r].reshape(128, 256), gb[:, 256 * r : 256 * r + 256])
+            dot_ = dot_.astype(BF).astype(F32)
+            do2 = two_heads(jnp.transpose(dot_).astype(BF))
+            share = L[l].share[0:1, 256 * i : 256 * i + 256]
+            head_row = lax.broadcasted_iota(I32, (128, 128), 0) < 64
+            scaled = dot_ * jnp.where(head_row, share[:, 0:128], share[:, 128:256])
+            R.do2[256 * i : 256 * i + 256, :] = two_heads(jnp.transpose(scaled).astype(BF))
+            prod = dot_ * L[l].ot[:, 128 * i : 128 * i + 128]
+            delta = jnp.concatenate(
+                [jnp.sum(prod[0:64], axis=0, keepdims=True), jnp.sum(prod[64:128], axis=0, keepdims=True)], axis=1
+            )
+            lanes = slice(256 * i, 256 * i + 256)
+            dqt = jnp.zeros((128, 256), F32)
+            for j in (2, 1, 3, 0):
+                zz = plus(z, j)
+                p = prob[4 * j : 4 * j + 4, :, lanes].reshape(512, 256)
+                dp = nt(values_of(l, zz), do2)
+                ds = (p.astype(F32) * ((dp - delta) * share)).astype(BF)
+                R.ds[j, :, lanes] = ds
+                if i == 1:
+                    p = prob[4 * j : 4 * j + 4].reshape(512, 512)
+                    dkv[zz, :, :, 0:128] = nn(R.ds[j], L[l].q2[...]).astype(BF).reshape(2, 256, 128)
+                    dkv[zz, :, :, 128:256] = nn(p, R.do2[...]).astype(BF).reshape(2, 256, 128)
+                    if j % 2:
+                        put(dkv.at[zz], L[l].dkvab.at[j // 2], dev(x, zz, y, k), ab[j])
+                    elif j:
+                        put(dkv.at[zz, mate], L[l].dkvc, partner, c_sem)
+                dqt += tn(keys_of(l, zz), ds)
+            dq.append(jnp.transpose(own_heads(dqt) * 0.125).astype(BF))
+        dq = jnp.concatenate(dq, axis=0)
+        gb = full(S[n].gb)
         gw = L[l].gwout
         otb = L[l].ot[...].astype(BF)
         for i in range(4):
             gw[i] = nn(otb, gb[:, 256 * i : 256 * i + 256]).astype(BF).reshape(4, 32, 256)
-        at = jnp.transpose(full(S[i0].a))
+        at = jnp.transpose(full(S[n].a))
         L[l].gwq[...] = nn(at, dq).astype(BF).reshape(4, 8, 32, 128)
         arrived(L[l].dkvc, c_sem)
         far = plus(z, 2)
@@ -621,8 +744,6 @@
         R.dkvf[...] = dkv[z].astype(F32) + got[0].astype(F32) + got[1].astype(F32)
         L[l].dkves[...] = R.dkvf[mate].astype(BF)
         put(L[l].dkves, L[l].dkve, partner, e_sem)
-        G[l].o = send_z(gw, L[l].rzout)
-        G[l].q = send_z(L[l].gwq, L[l].rzq)
         arrived(L[l].dkvd, d_sem)
         arrived(L[l].dkve, e_sem)
         tot = R.dkvf[yy] + L[l].dkvd[...].astype(F32) + L[l].dkve[...].astype(F32)
@@ -634,46 +755,69 @@
             R.dmh[...] = du
         else:
             du = (dvals + R.dmh[...].astype(F32)).astype(BF)
-        da = nt(jnp.concatenate([dq, dk], axis=1), L[l].wqk[...].reshape(1024, 256))
-        da += nt(du, L[l].wval[...].reshape(1024, 128))
-        rs = rs_start(4 + i0, da)
+        for i in streams:
+            rows = slice(128 * i, 128 * i + 128)
+            da = nt(jnp.concatenate([dq[rows], dk[rows]], axis=1), L[l].wqk[...].reshape(1024, 256))
+            da += nt(du[rows], L[l].wval[...].reshape(1024, 128))
+            rs_start(4 + n, i, da)
+        for i in streams:
+            rs_mid(4 + n, i)
         grads = nn(at, jnp.concatenate([dk, du], axis=1)).astype(BF)
         L[l].gwk[...] = grads[:, 0:128].reshape(4, 8, 32, 128)
         L[l].gwv[...] = grads[:, 128:256].reshape(4, 4, 2, 32, 128)
-        rs = rs_mid(4 + i0, rs)
         G[l].k = send_z(L[l].gwk, L[l].rzk)
+        G[l].o = send_z(L[l].gwout, L[l].rzout)
+        G[l].q = send_z(L[l].gwq, L[l].rzq)
         G[l].v = send_y(L[l].gwv, L[l].ryv)
-        hook1()
-        hook2()
-        return norm_backward(i0, rs_end(4 + i0, rs))
-
-    def feedforward_backward(l, hook1, hook2):
-        i0 = 2 * l + 1
-        gb = full(S[i0].gb)
-        wd = L[l].wdn
-        dhid = nt(gb[:, 0:256], wd[0].reshape(384, 256))
-        for i in range(1, 4):
-            dhid += nt(gb[:, 256 * i : 256 * i + 256], wd[i].reshape(384, 256))
-        gu = L[l].gu[...]
-        gate, up = gu[:, 0:384], gu[:, 384:768]
-        sig = jax.nn.sigmoid(gate)
-        dgate = dhid * up * sig * (1.0 + gate * (1.0 - sig))
-        dup = dhid * (gate * sig)
-        dgu = jnp.concatenate([dgate.astype(BF), dup.astype(BF)], axis=1)
-        rs = rs_start(4 + i0, nt(dgu, L[l].wgu[...].reshape(1024, 768)))
-        hook1()
-        rs = rs_mid(4 + i0, rs)
-        at = jnp.transpose(full(S[i0].a))
+        hook()
+
+    def feedforward_backward(l, states, hook):
+        n = 2 * l + 1
+
+        def work(i):
+            gb = S[n].gb[i].reshape(128, 1024)
+            wd = L[l].wdn
+            dhid = nt(gb[:, 0:256], wd[0].reshape(384, 256))
+            for r in range(1, 4):
+                dhid += nt(gb[:, 256 * r : 256 * r + 256], wd[r].reshape(384, 256))
+            gu = L[l].gu[128 * i : 128 * i + 128, :]
+            gate, up = gu[:, 0:384], gu[:, 384:768]
+            sig = jax.nn.sigmoid(gate)
+            dgate = dhid * up * sig * (1.0 + gate * (1.0 - sig))
+            dup = dhid * (gate * sig)
+            dgu = jnp.concatenate([dgate.astype(BF), dup.astype(BF)], axis=1)
+            R.dgu[i] = dgu
+            rs_start(4 + n, i, nt(dgu, L[l].wgu[...].reshape(1024, 768)))
+
+        opened(states, 4 + n, work)
+        at = jnp.transpose(full(S[n].a))
         gw = L[l].gwgu
-        gw[...] = nn(at, dgu).astype(BF).reshape(4, 4, 2, 32, 768)
-        G[l].g = send_y(gw, L[l].rygu)
+        gw[...] = nn(at, R.dgu[...].reshape(256, 768)).astype(BF).reshape(4, 4, 2, 32, 768)
+        far = plus(y, 2)
+        G[l].g = [new() for _ in range(4)]
+        put(gw.at[0:2, far], L[l].hygu.at[0], at_y(1), G[l].g[0])
+        put(gw.at[2:4, far], L[l].hygu.at[1], at_y(3), G[l].g[1])
+        gb = full(S[n].gb)
         ht = jnp.transpose(L[l].hid[...])
         gw = L[l].gwdn
         for i in range(4):
             gw[i] = nn(ht, gb[:, 256 * i : 256 * i + 256]).astype(BF).reshape(4, 96, 256)
-        G[l].d = send_z(gw, L[l].rzdn)
-        hook2()
-        return norm_backward(i0, rs_end(4 + i0, rs))
+        far = plus(z, 2)
+        G[l].d = [new() for _ in range(4)]
+        put(gw.at[far, 0:2], L[l].hzdn.at[0], at_z(1), G[l].d[0])
+        put(gw.at[far, 2:4], L[l].hzdn.at[1], at_z(3), G[l].d[1])
+        hook()
+
+    def ff_push(l):
+        gu, dn, hg, hd = L[l].gwgu, L[l].gwdn, L[l].hygu, L[l].hzdn
+        for h, j in ((0, 1), (1, 3)):
+            yd, zd, half = plus(y, j), plus(z, j), slice(2 * h, 2 * h + 2)
+            arrived(hg.at[h], G[l].g[h])
+            gu[half, yd] = (gu[half, yd].astype(F32) + hg[h].astype(F32)).astype(BF)
+            put(gu.at[:, yd], L[l].bygu.at[h], at_y(j), G[l].g[2 + h])
+            arrived(hd.at[h], G[l].d[h])
+            dn[zd, half] = (dn[zd, half].astype(F32) + hd[h].astype(F32)).astype(BF)
+            put(dn.at[zd], L[l].bzdn.at[h], at_z(j), G[l].d[2 + h])
 
     def summed(own, got):
         return own.astype(F32) + got[0].astype(F32) + got[1].astype(F32) + got[2].astype(F32)
@@ -707,8 +851,10 @@
         L[l].oo[...] = L[l].fout[...].astype(F32)
 
     def down_second(l):
-        arrived(L[l].rzdn, G[l].d)
-        L[l].sdn[...] = summed(L[l].gwdn[z], L[l].rzdn).astype(BF)
+        got = L[l].bzdn
+        arrived(got.at[0], G[l].d[2])
+        arrived(got.at[1], G[l].d[3])
+        L[l].sdn[...] = (L[l].gwdn[z].astype(F32) + got[0].astype(F32) + got[1].astype(F32)).astype(BF)
         G[l].d = rows_back(L[l].sdn, L[l].ydn)
 
     def down_third(l):
@@ -730,11 +876,7 @@
             put(st.at[2 * yd + kd], land.at[j], dev(x, z, yd, kd), sem)
         return sem
 
-    def rows_z(g, got, st, land, sem):
-        arrived(got, sem)
-        for i in range(4):
-            own = g[i, y].astype(F32) + got[0, i].astype(F32) + got[1, i].astype(F32) + got[2, i].astype(F32)
-            st[i] = own.astype(BF)
+    def rows_z(st, land):
         sem = new()
         land[0] = st[z, k]
         for j in (2, 6, 4, 3, 7, 5, 1):
@@ -755,10 +897,20 @@
         G[l].k = rows_y(L[l].gwk, L[l].rzk, L[l].sk, L[l].fk, G[l].k)
 
     def v_grad_second(l):
-        G[l].v = rows_z(L[l].gwv, L[l].ryv, L[l].sv, L[l].fv, G[l].v)
+        g, got, st = L[l].gwv, L[l].ryv, L[l].sv
+        arrived(got, G[l].v)
+        for i in range(4):
+            own = g[i, y].astype(F32) + got[0, i].astype(F32) + got[1, i].astype(F32) + got[2, i].astype(F32)
+            st[i] = own.astype(BF)
+        G[l].v = rows_z(st, L[l].fv)
 
     def gu_grad_second(l):
-        G[l].g = rows_z(L[l].gwgu, L[l].rygu, L[l].sgu, L[l].fgu, G[l].g)
+        g, got, st = L[l].gwgu, L[l].bygu, L[l].sgu
+        arrived(got.at[0], G[l].g[2])
+        arrived(got.at[1], G[l].g[3])
+        for i in range(4):
+            st[i] = (g[i, y].astype(F32) + got[0, i].astype(F32) + got[1, i].astype(F32)).astype(BF)
+        G[l].g = rows_z(st, L[l].fgu)
 
     def att_end(l):
         for land, result, sem in ((L[l].fq, L[l].oq, G[l].q), (L[l].fk, L[l].ok, G[l].k), (L[l].fv, L[l].ov, G[l].v)):
@@ -800,6 +952,8 @@
     for j in (1, 3, 2):
         put(R.gst, R.gx.at[j - 1], dev(plus(x, j), z, y, k), gx_sem)
     W[0].o = cross_first(L[0].wo, L[0].cwo)
+    pack_rest()
+    ff_first(0)
     arrived(R.gx, gx_sem)
     R.g1[...] = R.gst[...] + R.gx[0] + R.gx[1] + R.gx[2]
     gy_sem = new()
@@ -808,7 +962,6 @@
         put(R.g1, R.gyr.at[2 * y + k], dev(x, z, plus(y, j // 2), flip(j)), gy_sem)
     qk_second(0)
     v_second(0)
-    ff_first(0)
     W[0].o = cross_second(L[0].cwo, L[0].wout, W[0].o)
     arrived(R.gyr.at[0:7], gy_sem)
     for i in range(2):
@@ -816,53 +969,70 @@
     gz_sem = to_z(R.gz.at[z], R.gz.at[z])
     spread_rest(R.hin, in_sems)
     normed, _ = normalize(full(R.hin).astype(F32))
-    S[0].h[...] = R.hin[t]
+    for i in streams:
+        S[0].h[i] = R.hin[i, t]
+    gate_start(0)
     arrived(R.gz.at[0:3], gz_sem)
     R.gains[...] = jnp.concatenate([R.gz[i // 2, i % 2] for i in range(8)], axis=1)
-    S[0].a[...] = (normed * gain_row(0)).astype(BF).reshape(8, 32, 1024)
+    S[0].a[...] = (normed * gain_row(0)).astype(BF).reshape(2, 8, 16, 1024)
     W[0].o = cross_third(L[0].wout, W[0].o)
-    gate_second(0)
     W[0].d = cross_second(L[0].cwd, L[0].wdn, W[0].d)
     cot_sems = []
 
     def after_keys_0():
-        up_second(0)
-        W[0].d = cross_third(L[0].wdn, W[0].d)
+        ring_relay(W[0].gate)
+        up_start(0)
+        down_start(0)
+
+    def after_att_0():
         att_first(1)
         ff_first(1)
+
+    def in_gather_0():
+        ring_relay(W[0].up)
+        ring_relay(W[0].d)
 
     def in_ff_0():
         qk_second(1)
         v_second(1)
+
+    def after_ff_0():
         W[1].o = cross_second(L[1].cwo, L[1].wout, W[1].o)
-
-    def after_sum_1():
+        gate_start(1)
+        W[1].d = cross_second(L[1].cwd, L[1].wdn, W[1].d)
+
+    def in_gather_1():
         W[1].o = cross_third(L[1].wout, W[1].o)
-        gate_second(1)
-        W[1].d = cross_second(L[1].cwd, L[1].wdn, W[1].d)
 
     def after_keys_1():
-        up_second(1)
-        W[1].d = cross_third(L[1].wdn, W[1].d)
+        ring_relay(W[1].gate)
+        up_start(1)
+        down_start(1)
+
+    def after_att_1():
         cot_sems.append(spread_tokens(R.cot, S[3].gb))
 
-    def nothing():
-        pass
-
-    next_rows(0, attention_forward(0, after_keys_0))
-    next_rows(1, feedforward_forward(0, in_ff_0), after_sum_1)
-    next_rows(2, attention_forward(1, after_keys_1))
-    last = rs_mid(3, rs_start(3, feedforward_forward(1, lambda: spread_rest(S[3].gb, cot_sems[0]))))
-    S[3].gr[...] = S[3].gb[t]
-    out_sem = []
+    def in_gather_2():
+        ring_relay(W[1].up)
+        ring_relay(W[1].d)
+
+    def take_cotangent():
+        spread_rest(S[3].gb, cot_sems[0])
+        for i in streams:
+            S[3].gr[i] = S[3].gb[i, t]
+
+    landed = SimpleNamespace(out=new(), ing=new())
 
     def finish_outputs():
-        rows = (S[3].h[...].astype(F32) + rs_end(3, last)).astype(BF)
-        out_sem.append(to_owners(rows, R.outst, R.outrv))
-
-    def hand_back(i, rows):
-        S[i].gr[...] = rows
-        gather(S[i].gb, rows)
+        for i in streams:
+            rows = (S[3].h[i].astype(F32) + rs_end(3, i)).astype(BF)
+            to_owners(i, rows, R.outst, R.outrv, landed.out)
+
+    none = (None, None)
+    attention_forward(0, none, after_keys_0, after_att_0)
+    feedforward_forward(0, next_rows(0, in_gather_0), in_ff_0, after_ff_0)
+    attention_forward(1, next_rows(1, in_gather_1), after_keys_1, after_att_1)
+    feedforward_forward(1, next_rows(2, in_gather_2), nothing, take_cotangent)
 
     def ff_grads(l):
         gu_grad_second(l)
@@ -879,13 +1049,24 @@
         q_second(0)
         ff_grads(0)
 
-    hand_back(2, feedforward_backward(1, finish_outputs, nothing))
-    hand_back(1, attention_backward(1, lambda: ff_grads(1), nothing))
-    down_third(1)
-    hand_back(0, feedforward_backward(0, att_grads, lambda: gu_end(1)))
+    def after_grads_1():
+        att_grads()
+        gu_end(1)
+
+    def after_grads_0():
+        last_grads()
+        att_end(1)
+
+    feedforward_backward(1, none, finish_outputs)
+    states = hand_back(3, lambda: ff_push(1))
+    attention_backward(1, states, lambda: ff_grads(1))
+    states = hand_back(2, lambda: down_third(1))
+    feedforward_backward(0, states, after_grads_1)
+    states = hand_back(1, lambda: ff_push(0))
     out_third(1)
-    rows = attention_backward(0, last_grads, lambda: att_end(1))
-    in_grad_sem = to_owners(rows, R.ingst, R.ingrv)
+    attention_backward(0, states, after_grads_0)
+    for i in streams:
+        to_owners(i, norm_backward(0, i), R.ingst, R.ingrv, landed.ing)
     gg_sem = new()
     for j in (1, 3, 2):
         put(R.gg, R.ggx.at[j - 1], dev(plus(x, j), z, y, k), gg_sem)
@@ -904,7 +1085,7 @@
     out_end(1)
     down_end(1)
     gu_end(0)
-    arrived(R.outrv, out_sem[0])
+    arrived(R.outrv, landed.out)
     R.out[...] = R.outrv[...].reshape(2, 1, 64, 256)
     arrived(R.ggzr, gg_sem)
     gg = R.ggz[z] + R.ggzr[0] + R.ggzr[1] + R.ggzr[2]
@@ -915,7 +1096,7 @@
     for j in range(1, 8):
         yd = plus(y, j // 2)
         put(R.ggy.at[lax.div(yd, 2)], R.ggyr.at[j], dev(x, z, yd, flip(j)), gg_sem)
-    arrived(R.ingrv, in_grad_sem)
+    arrived(R.ingrv, landed.ing)
     R.ing[...] = R.ingrv[...].reshape(2, 1, 64, 256)
     att_end(0)
     out_end(0)
@@ -968,7 +1149,7 @@
 
 
 def body(inputs, cotangent, segment_ids, gains, *weights):
-    first = (inputs.reshape(2, 2, 32, 1024), cotangent.reshape(2, 2, 32, 1024), segment_ids, gains)
+    first = (inputs.reshape(2, 4, 16, 1024), cotangent.reshape(2, 4, 16, 1024), segment_ids, gains)
     results = call(*first, *weights)
     anywhere = pl.BlockSpec(memory_space=pl.ANY)
     return tuple(

time: 224 us -> 218 us (0.973)
  Pallas kernels: 220 us -> 215 us
    pallas_call x1, Pallas kernels: 218 us -> 213 us  [call(): pl.pallas_call(kernel, out_shape=[jax.ShapeDtypeStruct(shape, dtype) for...]
where the time goes in v2:
time: 218 us; the launch traced here: 216 us
  Pallas kernels  215 us (99%)
    pallas_call x1, Pallas kernels, call(): pl.pallas_call(kernel, out_shape=[jax.ShapeDtypeStruct(shape, dtype) for...  213 us

profile of v2, /device:TPU:4, one launch (start us, length us, event | category | flops | bytes accessed | tf_op | source)
XLA Modules:
  0.0 215.9 jit_solution(6419269827487476636)
XLA Ops:
  0.7 212.7 %shard_map.305 = (bf16[2,1,64,256]{3,2,1,0:T(8,128)(2,1)}, bf16[2,1,64,256]{3,2,1,0:T(8,128)(2,1)}, f32[1,32]{1,0:T(1,128)}, f32[32,256]{1,0:T(8,128)}, f32[32,2...) custom-call(bf16[2,4,16,1024]{3,2,1,0:T(8,128)(2,1)} %bitcast.2, ...), custom_call_target="tpu_custom_call" | custom-call | tf_op jit(solution)/shard_map/pallas_call | solution.py:1129
  213.3 2.4 %shard_map.306 = (bf16[2,1,64,256]{3,2,1,0:T(8,128)(2,1)}, bf16[2,1,64,256]{3,2,1,0:T(8,128)(2,1)}, f32[1,32]{1,0:T(1,128)}, f32[32,256]{1,0:T(8,128)}, f32[32,2...) custom-call(bf16[2,1,64,256]{3,2,1,0:T(8,128)(2,1)} %get-tuple-eleme, ...), custom_call_target="tpu_custom_call" | custom-call | tf_op jit(solution)/shard_map/pallas_call | solution.py:1156

commit v3 on v2

--- a/solution.py
+++ b/solution.py
@@ -19,19 +19,20 @@
     return shape, dtype
 
 
-LAYER_IN = dict(
+FAR_IN = dict(xin=spec(BF, 2, 4, 16, 1024), cot=spec(BF, 2, 4, 16, 1024))
+NEAR_IN = dict(seg=spec(I32, 2, 1, 2048), gains_in=spec(BF, 1, 32))
+FAR_LAYER_IN = dict(
     wq=spec(BF, 32, 256),
     wk=spec(BF, 32, 256),
     wv=spec(BF, 32, 256),
     wo=spec(BF, 32, 256),
     wg=spec(BF, 32, 704),
     wu=spec(BF, 32, 704),
-    wd=spec(BF, 88, 256),
 )
-COMMON_IN = dict(
-    xin=spec(BF, 2, 4, 16, 1024), cot=spec(BF, 2, 4, 16, 1024), seg=spec(I32, 2, 1, 2048), gains_in=spec(BF, 1, 32)
-)
-LAYER_OUT = dict(
+NEAR_LAYER_IN = dict(wd=spec(BF, 88, 256))
+FAR_OUT = dict(out=spec(BF, 2, 1, 64, 256), ing=spec(BF, 2, 1, 64, 256))
+NEAR_OUT = dict(ogg=spec(F32, 1, 32))
+FAR_LAYER_OUT = dict(
     oq=spec(F32, 32, 256),
     ok=spec(F32, 32, 256),
     ov=spec(F32, 32, 256),
@@ -40,7 +41,6 @@
     ou=spec(F32, 32, 704),
     od=spec(F32, 88, 256),
 )
-COMMON_OUT = dict(out=spec(BF, 2, 1, 64, 256), ing=spec(BF, 2, 1, 64, 256), ogg=spec(F32, 1, 32))
 COMMON = dict(
     hin=spec(BF, 2, 8, 16, 1024),
     pick=spec(BF, 704, 768),
@@ -57,7 +57,6 @@
     ggy=spec(F32, 2, 8, 128),
     ggyr=spec(F32, 8, 8, 128),
     scores=spec(F32, 16, 128, 512),
-    dkvf=spec(F32, 2, 256, 256),
     outst=spec(BF, 2, 4, 16, 256),
     ingst=spec(BF, 2, 4, 16, 256),
     outrv=spec(BF, 2, 64, 256),
@@ -136,30 +135,39 @@
     xs=spec(BF, 2, 3, 16, 1024),
     xr=spec(BF, 2, 3, 16, 1024),
 )
-N_SEM = 960
+N_SEM = 282
 N_LAYERS, N_SUB, N_EXCHANGE = 2, 4, 8
 
 
 def groups():
-    arguments = [(0, 0, COMMON_IN)] + [(1, l, LAYER_IN) for l in range(N_LAYERS)]
-    results = [(0, 0, COMMON_OUT)] + [(1, l, LAYER_OUT) for l in range(N_LAYERS)]
-    scratch = [(0, 0, COMMON)] + [(1, l, LAYER) for l in range(N_LAYERS)]
+    arguments = [(4, 0, FAR_IN), (0, 0, NEAR_IN)]
+    results = [(4, 0, FAR_OUT), (0, 0, NEAR_OUT)]
+    scratch = [(0, 0, COMMON), (0, 0, FAR_IN), (0, 0, FAR_OUT)]
+    for l in range(N_LAYERS):
+        arguments += [(5, l, FAR_LAYER_IN), (1, l, NEAR_LAYER_IN)]
+        results += [(5, l, FAR_LAYER_OUT)]
+        scratch += [(1, l, LAYER), (1, l, FAR_LAYER_IN), (1, l, FAR_LAYER_OUT)]
     scratch += [(2, i, SUB) for i in range(N_SUB)] + [(3, n, EXCHANGE) for n in range(N_EXCHANGE)]
     return arguments, results, scratch
 
 
 def named(refs):
-    spaces = [[SimpleNamespace() for _ in range(n)] for n in (1, N_LAYERS, N_SUB, N_EXCHANGE)]
+    spaces = [[SimpleNamespace() for _ in range(n)] for n in (1, N_LAYERS, N_SUB, N_EXCHANGE, 1, N_LAYERS)]
     left = list(refs)
     for group in groups():
         for kind, index, specs in group:
             for name in specs:
                 setattr(spaces[kind][index], name, left.pop(0))
-    return spaces[0][0], spaces[1], spaces[2], spaces[3]
+    return spaces[0][0], spaces[1], spaces[2], spaces[3], spaces[4][0], spaces[5]
 
 
 def specs_of(group):
     return [entry for _, _, specs in group for entry in specs.values()]
+
+
+def blocks_of(group):
+    spaces = [pl.ANY if kind >= 4 else pltpu.VMEM for kind, _, specs in group for _ in specs]
+    return [pl.BlockSpec(memory_space=space) for space in spaces]
 
 
 def nn(a, b):
@@ -180,10 +188,11 @@
 
 
 def kernel(*refs):
-    R, L, S, X = named(refs[:-1])
+    R, L, S, X, far_r, far_l = named(refs[:-1])
     sems = refs[-1]
     used = [0]
-    pending = []
+    pending, kept = [], []
+    outgoing = []
 
     def new():
         used[0] += 1
@@ -209,11 +218,13 @@
     sibling = dev(x, z, y, other)
 
     def put(src, dst, to, rsem):
+        if len(pending) % 32 == 0:
+            outgoing.append(new())
         copy = pltpu.make_async_remote_copy(
-            src_ref=src, dst_ref=dst, send_sem=new(), recv_sem=rsem, device_id=to, device_id_type=MESH
+            src_ref=src, dst_ref=dst, send_sem=outgoing[-1], recv_sem=rsem, device_id=to, device_id_type=MESH
         )
         copy.start()
-        pending.append((None, copy))
+        pending.append(copy)
 
     def put_or_keep(mine, src, dst, to, rsem):
         copy = pltpu.make_async_remote_copy(
@@ -228,7 +239,7 @@
         def _():
             copy.start()
 
-        pending.append((mine, copy))
+        kept.append((mine, copy))
 
     def arrived(ref, sem):
         pltpu.make_async_copy(ref, ref, sem).wait()
@@ -255,6 +266,29 @@
     @pl.when(x != z)
     def _():
         greet(dev(z, x, y, k))
+
+    def fetch(src, dst):
+        copy = pltpu.make_async_copy(src, dst, new())
+        copy.start()
+        return copy
+
+    def fetch_att(l):
+        ends = ((far_l[l].wq, L[l].wq), (far_l[l].wk, L[l].wk), (far_l[l].wv, L[l].wv), (far_l[l].wo, L[l].wo))
+        return [fetch(src, dst) for src, dst in ends]
+
+    def wait_for(copies):
+        for copy in copies:
+            copy.wait()
+
+    coming = fetch_att(0)
+    xin_coming = fetch(far_r.xin, R.xin)
+    later = fetch_att(1) + [fetch(far_r.cot, R.cot)]
+    for l in range(2):
+        later += [fetch(far_l[l].wg, L[l].wg), fetch(far_l[l].wu, L[l].wu)]
+    leaving = []
+
+    def leave(src, dst):
+        leaving.append(fetch(src, dst))
 
     def pack_att(l):
         for i in range(2):
@@ -282,6 +316,7 @@
         pack_att(1)
         R.gg[...] = jnp.zeros((8, 1024), F32)
 
+    wait_for(coming)
     pack_att(0)
     column = lax.broadcasted_iota(I32, (32, 128), 1) - 32 * lax.rem(c, 4)
     spot = (lax.broadcasted_iota(I32, (32, 128), 0) == column).astype(F32).astype(BF)
@@ -398,40 +433,36 @@
         pb, sib = X[n].pb, X[n].sib
         for r in range(8):
             pb[i, r % 2, r // 2] = part[16 * r : 16 * r + 16].astype(BF)
-        sem = sums[n, i] = [new() for _ in range(4)]
+        sem = sums[n, i] = new()
         for j in (1, 3, 2, 0):
             xd = plus(x, j)
-            put(pb.at[i, other, xd], sib.at[i, xd], sibling, sem[j])
+            put(pb.at[i, other, xd], sib.at[i, xd], sibling, sem)
 
     def rs_mid(n, i):
         pb, sib, xs, xr = X[n].pb, X[n].sib, X[n].xs, X[n].xr
-        sem, out = sums[n, i], []
+        arrived(sib.at[i], sums[n, i])
+        sem = sums[n, i] = new()
         for j in (1, 3, 2):
             xd = plus(x, j)
-            arrived(sib.at[i, xd], sem[j])
             xs[i, j - 1] = (pb[i, k, xd].astype(F32) + sib[i, xd].astype(F32)).astype(BF)
-            out.append(new())
-            put(xs.at[i, j - 1], xr.at[i, j - 1], dev(xd, z, y, k), out[-1])
-        sums[n, i] = sem[0], out
+            put(xs.at[i, j - 1], xr.at[i, j - 1], dev(xd, z, y, k), sem)
 
     def rs_end(n, i):
         pb, sib, xr = X[n].pb, X[n].sib, X[n].xr
-        own, out = sums[n, i]
-        arrived(sib.at[i, x], own)
         total = pb[i, k, x].astype(F32) + sib[i, x].astype(F32)
-        for j, sem in zip((1, 3, 2), out):
-            arrived(xr.at[i, j - 1], sem)
+        arrived(xr.at[i], sums[n, i])
+        for j in (1, 3, 2):
             total += xr[i, j - 1].astype(F32)
         return total
 
     def gather_start(buf, i, block):
         buf[i, t] = block
         mine = buf.at[i, t]
-        rx = [new() for _ in range(4)]
-        rk = [new() for _ in range(4)]
+        rx = {j: new() for j in (1, 3, 2)}
+        rk = new()
         for j in (1, 3, 2):
             put(mine, mine, dev(plus(x, j), z, y, k), rx[j])
-        put(mine, mine, sibling, rk[0])
+        put(mine, mine, sibling, rk)
         return buf, i, rx, rk
 
     def gather_forward(state):
@@ -440,13 +471,12 @@
             for j in (1, 3, 2):
                 slot = buf.at[i, 2 * plus(x, 4 - j) + k]
                 arrived(slot, rx[j])
-                put(slot, slot, sibling, rk[j])
+                put(slot, slot, sibling, rk)
 
     def gather_finish(state):
         if state is not None:
             buf, i, rx, rk = state
-            for j in range(4):
-                arrived(buf.at[i, 0], rk[j])
+            arrived(buf.at[i, 0:4], rk)
 
     def nothing():
         pass
@@ -530,7 +560,7 @@
 
     def attention_forward(l, states, hook, late):
         kv = L[l].kv
-        direct, relayed = [[new() for _ in range(4)] for _ in streams], [[new() for _ in range(4)] for _ in streams]
+        direct, relayed = ([{j: new() for j in (1, 2, 3)} for _ in streams] for _ in range(2))
         from_mate = [new() for _ in streams]
         for i in streams:
             if i == 1:
@@ -572,6 +602,8 @@
                     arrived(kv.at[zz, mate, i], relayed[i][4 - j])
                 elif j:
                     arrived(kv.at[zz, mate, i], relayed[i][2])
+            if j == 1:
+                hook()
             scores[4 * j : 4 * j + 4] = nt(keys_of(l, zz), L[l].q2[...]).reshape(4, 128, 512)
 
             def mask(i, top, j=j, zz=zz):
@@ -589,7 +621,6 @@
                     opposite = kv.at[plus(z, 2), yy, i]
                     arrived(opposite, direct[i][2])
                     put(opposite, opposite, partner, relayed[i][2])
-        hook()
         prob = L[l].prob
         for i in streams:
             lanes = slice(256 * i, 256 * i + 256)
@@ -687,7 +718,7 @@
     def attention_backward(l, states, hook):
         n = 2 * l
         wo, dkv, prob = L[l].wout, L[l].dkv, L[l].prob
-        ab, c_sem = [new() for _ in range(4)], new()
+        ab, own_ab, c_sem = {j: new() for j in (1, 3)}, {j: new() for j in (1, 3)}, new()
         dq = []
         for i in streams:
             if i == 1:
@@ -720,33 +751,38 @@
                     dkv[zz, :, :, 0:128] = nn(R.ds[j], L[l].q2[...]).astype(BF).reshape(2, 256, 128)
                     dkv[zz, :, :, 128:256] = nn(p, R.do2[...]).astype(BF).reshape(2, 256, 128)
                     if j % 2:
-                        put(dkv.at[zz], L[l].dkvab.at[j // 2], dev(x, zz, y, k), ab[j])
+                        put(dkv.at[zz, mate], L[l].dkvab.at[j // 2, mate], dev(x, zz, y, k), ab[j])
                     elif j:
                         put(dkv.at[zz, mate], L[l].dkvc, partner, c_sem)
                 dqt += tn(keys_of(l, zz), ds)
+                if i == 1 and j == 3:
+                    for r in (1, 3):
+                        put(dkv.at[plus(z, r), yy], L[l].dkvab.at[r // 2, yy], dev(x, plus(z, r), y, k), own_ab[r])
             dq.append(jnp.transpose(own_heads(dqt) * 0.125).astype(BF))
         dq = jnp.concatenate(dq, axis=0)
         gb = full(S[n].gb)
+        arrived(L[l].dkvc, c_sem)
+        far = plus(z, 2)
+        L[l].dkvds[...] = (dkv[far, yy].astype(F32) + L[l].dkvc[...].astype(F32)).astype(BF)
+        d_sem, e_sem = new(), new()
+        put(L[l].dkvds, L[l].dkvd, dev(x, far, y, k), d_sem)
+        got = L[l].dkvab
+        arrived(got.at[0, mate], ab[1])
+        arrived(got.at[1, mate], ab[3])
+        L[l].dkves[...] = (dkv[z, mate].astype(F32) + got[0, mate].astype(F32) + got[1, mate].astype(F32)).astype(BF)
+        put(L[l].dkves, L[l].dkve, partner, e_sem)
         gw = L[l].gwout
         otb = L[l].ot[...].astype(BF)
         for i in range(4):
             gw[i] = nn(otb, gb[:, 256 * i : 256 * i + 256]).astype(BF).reshape(4, 32, 256)
         at = jnp.transpose(full(S[n].a))
         L[l].gwq[...] = nn(at, dq).astype(BF).reshape(4, 8, 32, 128)
-        arrived(L[l].dkvc, c_sem)
-        far = plus(z, 2)
-        L[l].dkvds[...] = (dkv[far, yy].astype(F32) + L[l].dkvc[...].astype(F32)).astype(BF)
-        d_sem, e_sem = new(), new()
-        put(L[l].dkvds, L[l].dkvd, dev(x, far, y, k), d_sem)
-        got = L[l].dkvab
-        arrived(got.at[0], ab[1])
-        arrived(got.at[1], ab[3])
-        R.dkvf[...] = dkv[z].astype(F32) + got[0].astype(F32) + got[1].astype(F32)
-        L[l].dkves[...] = R.dkvf[mate].astype(BF)
-        put(L[l].dkves, L[l].dkve, partner, e_sem)
+        arrived(got.at[0, yy], own_ab[1])
+        arrived(got.at[1, yy], own_ab[3])
+        tot = dkv[z, yy].astype(F32) + got[0, yy].astype(F32) + got[1, yy].astype(F32)
         arrived(L[l].dkvd, d_sem)
         arrived(L[l].dkve, e_sem)
-        tot = R.dkvf[yy] + L[l].dkvd[...].astype(F32) + L[l].dkve[...].astype(F32)
+        tot = tot + L[l].dkvd[...].astype(F32) + L[l].dkve[...].astype(F32)
         dk = tot[:, 0:128].astype(BF)
         dvals = tot[:, 128:256]
         if l == 1:
@@ -755,6 +791,15 @@
             R.dmh[...] = du
         else:
             du = (dvals + R.dmh[...].astype(F32)).astype(BF)
+        def send_grads():
+            grads = nn(at, jnp.concatenate([dk, du], axis=1)).astype(BF)
+            L[l].gwk[...] = grads[:, 0:128].reshape(4, 8, 32, 128)
+            L[l].gwv[...] = grads[:, 128:256].reshape(4, 4, 2, 32, 128)
+            G[l].k = send_z(L[l].gwk, L[l].rzk)
+            G[l].v = send_y(L[l].gwv, L[l].ryv)
+
+        if l == 0:
+            send_grads()
         for i in streams:
             rows = slice(128 * i, 128 * i + 128)
             da = nt(jnp.concatenate([dq[rows], dk[rows]], axis=1), L[l].wqk[...].reshape(1024, 256))
@@ -762,13 +807,10 @@
             rs_start(4 + n, i, da)
         for i in streams:
             rs_mid(4 + n, i)
-        grads = nn(at, jnp.concatenate([dk, du], axis=1)).astype(BF)
-        L[l].gwk[...] = grads[:, 0:128].reshape(4, 8, 32, 128)
-        L[l].gwv[...] = grads[:, 128:256].reshape(4, 4, 2, 32, 128)
-        G[l].k = send_z(L[l].gwk, L[l].rzk)
+        if l == 1:
+            send_grads()
         G[l].o = send_z(L[l].gwout, L[l].rzout)
         G[l].q = send_z(L[l].gwq, L[l].rzq)
-        G[l].v = send_y(L[l].gwv, L[l].ryv)
         hook()
 
     def feedforward_backward(l, states, hook):
@@ -849,6 +891,7 @@
     def out_end(l):
         arrived(L[l].fout, G[l].o)
         L[l].oo[...] = L[l].fout[...].astype(F32)
+        leave(L[l].oo, far_l[l].oo)
 
     def down_second(l):
         got = L[l].bzdn
@@ -865,6 +908,7 @@
     def down_end(l):
         arrived(L[l].fdn, G[l].d)
         L[l].od[...] = L[l].fdn[0:88, :].astype(F32)
+        leave(L[l].od, far_l[l].od)
 
     def rows_y(g, got, st, land, sem):
         arrived(got, sem)
@@ -913,10 +957,16 @@
         G[l].g = rows_z(st, L[l].fgu)
 
     def att_end(l):
-        for land, result, sem in ((L[l].fq, L[l].oq, G[l].q), (L[l].fk, L[l].ok, G[l].k), (L[l].fv, L[l].ov, G[l].v)):
+        f = far_l[l]
+        for land, result, sem, to in (
+            (L[l].fq, L[l].oq, G[l].q, f.oq),
+            (L[l].fk, L[l].ok, G[l].k, f.ok),
+            (L[l].fv, L[l].ov, G[l].v, f.ov),
+        ):
             low, high = halves(land, sem)
             result[:, 0:128] = low
             result[:, 128:256] = high
+            leave(result, to)
 
     def gu_end(l):
         low, high = halves(L[l].fgu, G[l].g)
@@ -932,6 +982,8 @@
         both = nt(main, R.pick[...]) + nt(rest, R.pick[...])
         L[l].og[...] = both[0:32]
         L[l].ou[...] = both[32:64]
+        leave(L[l].og, far_l[l].og)
+        leave(L[l].ou, far_l[l].ou)
 
     def nothing():
         pass
@@ -947,11 +999,13 @@
 
     qk_first(0)
     W[0].v = z_first(L[0].vst, L[0].wval)
+    xin_coming.wait()
     in_sems = spread_tokens(R.xin, R.hin)
     gx_sem = new()
     for j in (1, 3, 2):
         put(R.gst, R.gx.at[j - 1], dev(plus(x, j), z, y, k), gx_sem)
     W[0].o = cross_first(L[0].wo, L[0].cwo)
+    wait_for(later)
     pack_rest()
     ff_first(0)
     arrived(R.gx, gx_sem)
@@ -1087,6 +1141,7 @@
     gu_end(0)
     arrived(R.outrv, landed.out)
     R.out[...] = R.outrv[...].reshape(2, 1, 64, 256)
+    leave(R.out, far_r.out)
     arrived(R.ggzr, gg_sem)
     gg = R.ggz[z] + R.ggzr[0] + R.ggzr[1] + R.ggzr[2]
     R.ggy[0] = gg[:, 0:128]
@@ -1098,6 +1153,7 @@
         put(R.ggy.at[lax.div(yd, 2)], R.ggyr.at[j], dev(x, z, yd, flip(j)), gg_sem)
     arrived(R.ingrv, landed.ing)
     R.ing[...] = R.ingrv[...].reshape(2, 1, 64, 256)
+    leave(R.ing, far_r.ing)
     att_end(0)
     out_end(0)
     down_end(0)
@@ -1111,27 +1167,26 @@
     for i in range(4):
         gain += jnp.where(part == i, gg[:, 32 * i : 32 * i + 32], 0.0)
     R.ogg[...] = gain
-    for mine, copy in pending:
-        if mine is None:
+    wait_for(leaving)
+    for copy in pending:
+        copy.wait_send()
+    for mine, copy in kept:
+
+        @pl.when(jnp.logical_not(mine))
+        def _(copy=copy):
             copy.wait_send()
-        else:
-
-            @pl.when(jnp.logical_not(mine))
-            def _(copy=copy):
-                copy.wait_send()
 
     assert used[0] <= N_SEM, used
 
 
 def call(*args):
-    whole = pl.BlockSpec(memory_space=pltpu.VMEM)
-    arguments, results, scratch = (specs_of(group) for group in groups())
+    arguments, results, scratch = groups()
     return pl.pallas_call(
         kernel,
-        out_shape=[jax.ShapeDtypeStruct(shape, dtype) for shape, dtype in results],
-        in_specs=[whole] * len(arguments),
-        out_specs=[whole] * len(results),
-        scratch_shapes=[pltpu.VMEM(shape, dtype) for shape, dtype in scratch]
+        out_shape=[jax.ShapeDtypeStruct(shape, dtype) for shape, dtype in specs_of(results)],
+        in_specs=blocks_of(arguments),
+        out_specs=blocks_of(results),
+        scratch_shapes=[pltpu.VMEM(shape, dtype) for shape, dtype in specs_of(scratch)]
         + [pltpu.SemaphoreType.DMA((N_SEM,))],
         compiler_params=pltpu.CompilerParams(
             collective_id=0, has_side_effects=True, vmem_limit_bytes=62 * 1024 * 1024

time: 218 us -> 205 us (0.940)
  Pallas kernels: 215 us -> 201 us
    pallas_call x1, Pallas kernels: 213 us -> 199 us  [call(): pl.pallas_call(kernel, out_shape=[jax.ShapeDtypeStruct(shape, dtype) for...]
where the time goes in v3:
time: 205 us; the launch traced here: 202 us
  Pallas kernels  201 us (98%)
    pallas_call x1, Pallas kernels, call(): pl.pallas_call(kernel, out_shape=[jax.ShapeDtypeStruct(shape, dtype) for...  199 us

profile of v3, /device:TPU:4, one launch (start us, length us, event | category | flops | bytes accessed | tf_op | source)
XLA Modules:
  0.0 201.9 jit_solution(11695573138566718802)
XLA Ops:
  0.7 198.7 %shard_map.305 = (bf16[2,1,64,256]{3,2,1,0:T(8,128)(2,1)}, bf16[2,1,64,256]{3,2,1,0:T(8,128)(2,1)}, f32[1,32]{1,0:T(1,128)}, f32[32,256]{1,0:T(8,128)}, f32[32,2...) custom-call(bf16[2,4,16,1024]{3,2,1,0:T(8,128)(2,1)} %bitcast.2, ...), custom_call_target="tpu_custom_call" | custom-call | tf_op jit(solution)/shard_map/pallas_call | solution.py:1184
  199.3 2.4 %shard_map.306 = (bf16[2,1,64,256]{3,2,1,0:T(8,128)(2,1)}, bf16[2,1,64,256]{3,2,1,0:T(8,128)(2,1)}, f32[1,32]{1,0:T(1,128)}, f32[32,256]{1,0:T(8,128)}, f32[32,2...) custom-call(bf16[2,1,64,256]{3,2,1,0:T(8,128)(2,1)} %get-tuple-eleme, ...), custom_call_target="tpu_custom_call" | custom-call | tf_op jit(solution)/shard_map/pallas_call | solution.py:1211

commit v4 on v3

--- a/solution.py
+++ b/solution.py
@@ -50,6 +50,7 @@
     gyr=spec(F32, 8, 8, 128),
     gz=spec(F32, 4, 2, 8, 128),
     gains=spec(F32, 8, 1024),
+    normed=spec(F32, 256, 1024),
     gg=spec(F32, 8, 1024),
     ggx=spec(F32, 3, 8, 1024),
     ggz=spec(F32, 4, 8, 256),
@@ -91,30 +92,26 @@
     dkvd=spec(BF, 256, 256),
     dkves=spec(BF, 256, 256),
     dkve=spec(BF, 256, 256),
-    gwq=spec(BF, 4, 8, 32, 128),
     gwk=spec(BF, 4, 8, 32, 128),
-    gwv=spec(BF, 4, 4, 2, 32, 128),
+    gwv=spec(BF, 4, 4, 2, 32, 256),
     gwout=spec(BF, 4, 4, 32, 256),
     gwgu=spec(BF, 4, 4, 2, 32, 768),
     gwdn=spec(BF, 4, 4, 96, 256),
-    rzq=spec(BF, 3, 8, 32, 128),
     rzk=spec(BF, 3, 8, 32, 128),
-    ryv=spec(BF, 3, 4, 2, 32, 128),
+    ryv=spec(BF, 3, 4, 2, 32, 256),
     rzout=spec(BF, 3, 4, 32, 256),
     hygu=spec(BF, 2, 2, 2, 32, 768),
     bygu=spec(BF, 2, 4, 2, 32, 768),
     hzdn=spec(BF, 2, 2, 96, 256),
     bzdn=spec(BF, 2, 4, 96, 256),
     share=spec(F32, 8, 512),
-    sq=spec(BF, 8, 32, 128),
     sk=spec(BF, 8, 32, 128),
-    sv=spec(BF, 4, 2, 32, 128),
+    sv=spec(BF, 4, 2, 32, 256),
     sout=spec(BF, 4, 32, 256),
     sgu=spec(BF, 4, 2, 32, 768),
     sdn=spec(BF, 4, 96, 256),
-    fq=spec(BF, 8, 32, 128),
     fk=spec(BF, 8, 32, 128),
-    fv=spec(BF, 8, 32, 128),
+    fv=spec(BF, 8, 32, 256),
     fgu=spec(BF, 8, 32, 768),
     yout=spec(BF, 4, 32, 256),
     ydn=spec(BF, 4, 96, 256),
@@ -375,14 +372,18 @@
     def at_z(j):
         return dev(x, plus(z, j), y, k)
 
-    def ring_start(block, v, at):
+    def ring_start(block, v, at, direct=False):
         sems_ = [new() for _ in range(4)]
         put(block(v), block(v), at(1), sems_[0])
         put(block(v), block(v), at(3), sems_[1])
-        return block, v, at, sems_
+        if direct:
+            put(block(v), block(v), at(2), sems_[2])
+        return block, v, at, sems_, direct
 
     def ring_relay(state):
-        block, v, at, sems_ = state
+        block, v, at, sems_, direct = state
+        if direct:
+            return
         before, after = plus(v, 3), plus(v, 1)
         arrived(block(before), sems_[0])
         put(block(before, 0), block(before, 0), at(1), sems_[2])
@@ -390,8 +391,13 @@
         put(block(after, 1), block(after, 1), at(3), sems_[3])
 
     def ring_end(state):
-        block, v, at, sems_ = state
+        block, v, at, sems_, direct = state
         far = plus(v, 2)
+        if direct:
+            arrived(block(plus(v, 3)), sems_[0])
+            arrived(block(plus(v, 1)), sems_[1])
+            arrived(block(far), sems_[2])
+            return
         arrived(block(far, 0), sems_[2])
         arrived(block(far, 1), sems_[3])
 
@@ -407,7 +413,7 @@
 
     def down_start(l):
         arrived(L[l].wdn.at[z], W[l].d)
-        W[l].d = ring_start(lambda v, h=None: L[l].wdn.at[v, halved(h)], z, at_z)
+        W[l].d = ring_start(lambda v, h=None: L[l].wdn.at[v, halved(h)], z, at_z, True)
 
     def cross_first(src, dst):
         sem = new()
@@ -685,7 +691,9 @@
         da = rs_end(4 + n, i)
         normed, inverse = normalize(S[n].h[i].astype(F32))
         gain_part = jnp.sum(da * normed, axis=0, keepdims=True)
-        if i == 0:
+        if n == 0:
+            pass
+        elif i == 0:
             R.gg[n : n + 1, :] = gain_part
         else:
             R.gg[n : n + 1, :] += gain_part
@@ -776,7 +784,6 @@
         for i in range(4):
             gw[i] = nn(otb, gb[:, 256 * i : 256 * i + 256]).astype(BF).reshape(4, 32, 256)
         at = jnp.transpose(full(S[n].a))
-        L[l].gwq[...] = nn(at, dq).astype(BF).reshape(4, 8, 32, 128)
         arrived(got.at[0, yy], own_ab[1])
         arrived(got.at[1, yy], own_ab[3])
         tot = dkv[z, yy].astype(F32) + got[0, yy].astype(F32) + got[1, yy].astype(F32)
@@ -792,9 +799,9 @@
         else:
             du = (dvals + R.dmh[...].astype(F32)).astype(BF)
         def send_grads():
-            grads = nn(at, jnp.concatenate([dk, du], axis=1)).astype(BF)
-            L[l].gwk[...] = grads[:, 0:128].reshape(4, 8, 32, 128)
-            L[l].gwv[...] = grads[:, 128:256].reshape(4, 4, 2, 32, 128)
+            grads = nn(at, jnp.concatenate([dq, du, dk], axis=1)).astype(BF)
+            L[l].gwv[...] = grads[:, 0:256].reshape(4, 4, 2, 32, 256)
+            L[l].gwk[...] = grads[:, 256:384].reshape(4, 8, 32, 128)
             G[l].k = send_z(L[l].gwk, L[l].rzk)
             G[l].v = send_y(L[l].gwv, L[l].ryv)
 
@@ -805,12 +812,20 @@
             da = nt(jnp.concatenate([dq[rows], dk[rows]], axis=1), L[l].wqk[...].reshape(1024, 256))
             da += nt(du[rows], L[l].wval[...].reshape(1024, 128))
             rs_start(4 + n, i, da)
+            if l == 0:
+                gain_part = jnp.sum(da * R.normed[rows, :], axis=0, keepdims=True)
+                if i == 0:
+                    R.gg[0:1, :] = gain_part
+                else:
+                    R.gg[0:1, :] += gain_part
+        if l == 0:
+            for j in (1, 3, 2):
+                put(R.gg, R.ggx.at[j - 1], dev(plus(x, j), z, y, k), landed.gx)
         for i in streams:
             rs_mid(4 + n, i)
         if l == 1:
             send_grads()
         G[l].o = send_z(L[l].gwout, L[l].rzout)
-        G[l].q = send_z(L[l].gwq, L[l].rzq)
         hook()
 
     def feedforward_backward(l, states, hook):
@@ -929,13 +944,11 @@
         return sem
 
     def halves(land, sem):
-        arrived(land.at[1:8], sem)
+        if sem is not None:
+            arrived(land.at[1:8], sem)
         own = land[0].astype(F32) + land[2].astype(F32) + land[4].astype(F32) + land[6].astype(F32)
         far = land[1].astype(F32) + land[3].astype(F32) + land[5].astype(F32) + land[7].astype(F32)
         return jnp.where(k == 0, own, far), jnp.where(k == 0, far, own)
-
-    def q_second(l):
-        G[l].q = rows_y(L[l].gwq, L[l].rzq, L[l].sq, L[l].fq, G[l].q)
 
     def k_second(l):
         G[l].k = rows_y(L[l].gwk, L[l].rzk, L[l].sk, L[l].fk, G[l].k)
@@ -958,10 +971,11 @@
 
     def att_end(l):
         f = far_l[l]
+        arrived(L[l].fv.at[1:8], G[l].v)
         for land, result, sem, to in (
-            (L[l].fq, L[l].oq, G[l].q, f.oq),
             (L[l].fk, L[l].ok, G[l].k, f.ok),
-            (L[l].fv, L[l].ov, G[l].v, f.ov),
+            (L[l].fv.at[:, :, 0:128], L[l].oq, None, f.oq),
+            (L[l].fv.at[:, :, 128:256], L[l].ov, None, f.ov),
         ):
             low, high = halves(land, sem)
             result[:, 0:128] = low
@@ -1023,6 +1037,7 @@
     gz_sem = to_z(R.gz.at[z], R.gz.at[z])
     spread_rest(R.hin, in_sems)
     normed, _ = normalize(full(R.hin).astype(F32))
+    R.normed[...] = normed
     for i in streams:
         S[0].h[i] = R.hin[i, t]
     gate_start(0)
@@ -1037,8 +1052,6 @@
         ring_relay(W[0].gate)
         up_start(0)
         down_start(0)
-
-    def after_att_0():
         att_first(1)
         ff_first(1)
 
@@ -1075,7 +1088,7 @@
         for i in streams:
             S[3].gr[i] = S[3].gb[i, t]
 
-    landed = SimpleNamespace(out=new(), ing=new())
+    landed = SimpleNamespace(out=new(), ing=new(), gx=new())
 
     def finish_outputs():
         for i in streams:
@@ -1083,7 +1096,7 @@
             to_owners(i, rows, R.outst, R.outrv, landed.out)
 
     none = (None, None)
-    attention_forward(0, none, after_keys_0, after_att_0)
+    attention_forward(0, none, after_keys_0, nothing)
     feedforward_forward(0, next_rows(0, in_gather_0), in_ff_0, after_ff_0)
     attention_forward(1, next_rows(1, in_gather_1), after_keys_1, after_att_1)
     feedforward_forward(1, next_rows(2, in_gather_2), nothing, take_cotangent)
@@ -1094,13 +1107,10 @@
 
     def att_grads():
         out_second(1)
-        q_second(1)
         k_second(1)
         v_grad_second(1)
 
     def last_grads():
-        out_second(0)
-        q_second(0)
         ff_grads(0)
 
     def after_grads_1():
@@ -1119,16 +1129,7 @@
     states = hand_back(1, lambda: ff_push(0))
     out_third(1)
     attention_backward(0, states, after_grads_0)
-    for i in streams:
-        to_owners(i, norm_backward(0, i), R.ingst, R.ingrv, landed.ing)
-    gg_sem = new()
-    for j in (1, 3, 2):
-        put(R.gg, R.ggx.at[j - 1], dev(plus(x, j), z, y, k), gg_sem)
-    k_second(0)
-    v_grad_second(0)
-    out_third(0)
-    down_third(0)
-    arrived(R.ggx, gg_sem)
+    arrived(R.ggx, landed.gx)
     gg = R.gg[...] + R.ggx[0] + R.ggx[1] + R.ggx[2]
     for i in range(4):
         R.ggz[i] = gg[:, 256 * i : 256 * i + 256]
@@ -1136,12 +1137,8 @@
     for j in (1, 3, 2):
         zd = plus(z, j)
         put(R.ggz.at[zd], R.ggzr.at[j - 1], dev(x, zd, y, k), gg_sem)
-    out_end(1)
-    down_end(1)
-    gu_end(0)
-    arrived(R.outrv, landed.out)
-    R.out[...] = R.outrv[...].reshape(2, 1, 64, 256)
-    leave(R.out, far_r.out)
+    for i in streams:
+        to_owners(i, norm_backward(0, i), R.ingst, R.ingrv, landed.ing)
     arrived(R.ggzr, gg_sem)
     gg = R.ggz[z] + R.ggzr[0] + R.ggzr[1] + R.ggzr[2]
     R.ggy[0] = gg[:, 0:128]
@@ -1151,6 +1148,17 @@
     for j in range(1, 8):
         yd = plus(y, j // 2)
         put(R.ggy.at[lax.div(yd, 2)], R.ggyr.at[j], dev(x, z, yd, flip(j)), gg_sem)
+    k_second(0)
+    v_grad_second(0)
+    out_second(0)
+    down_third(0)
+    out_third(0)
+    out_end(1)
+    down_end(1)
+    gu_end(0)
+    arrived(R.outrv, landed.out)
+    R.out[...] = R.outrv[...].reshape(2, 1, 64, 256)
+    leave(R.out, far_r.out)
     arrived(R.ingrv, landed.ing)
     R.ing[...] = R.ingrv[...].reshape(2, 1, 64, 256)
     leave(R.ing, far_r.ing)

time: 205 us -> 200 us (0.976); the launches traced: 202 us -> 200 us
  no operation moved by 1% of the time
where the time goes in v4:
time: 200 us
  Pallas kernels  199 us (100%)
    pallas_call x1, Pallas kernels, call(): pl.pallas_call(kernel, out_shape=[jax.ShapeDtypeStruct(shape, dtype) for...  197 us

profile of v4, /device:TPU:4, one launch (start us, length us, event | category | flops | bytes accessed | tf_op | source)
XLA Modules:
  0.0 200.0 jit_solution(4201124484876113441)
XLA Ops:
  0.7 196.8 %shard_map.305 = (bf16[2,1,64,256]{3,2,1,0:T(8,128)(2,1)}, bf16[2,1,64,256]{3,2,1,0:T(8,128)(2,1)}, f32[1,32]{1,0:T(1,128)}, f32[32,256]{1,0:T(8,128)}, f32[32,2...) custom-call(bf16[2,4,16,1024]{3,2,1,0:T(8,128)(2,1)} %bitcast.2, ...), custom_call_target="tpu_custom_call" | custom-call | tf_op jit(solution)/shard_map/pallas_call | solution.py:1192
  197.4 2.4 %shard_map.306 = (bf16[2,1,64,256]{3,2,1,0:T(8,128)(2,1)}, bf16[2,1,64,256]{3,2,1,0:T(8,128)(2,1)}, f32[1,32]{1,0:T(1,128)}, f32[32,256]{1,0:T(8,128)}, f32[32,2...) custom-call(bf16[2,1,64,256]{3,2,1,0:T(8,128)(2,1)} %get-tuple-eleme, ...), custom_call_target="tpu_custom_call" | custom-call | tf_op jit(solution)/shard_map/pallas_call | solution.py:1219

commit v5 on v4

--- a/solution.py
+++ b/solution.py
@@ -784,6 +784,8 @@
         for i in range(4):
             gw[i] = nn(otb, gb[:, 256 * i : 256 * i + 256]).astype(BF).reshape(4, 32, 256)
         at = jnp.transpose(full(S[n].a))
+        if l == 0:
+            G[l].o = send_z(L[l].gwout, L[l].rzout)
         arrived(got.at[0, yy], own_ab[1])
         arrived(got.at[1, yy], own_ab[3])
         tot = dkv[z, yy].astype(F32) + got[0, yy].astype(F32) + got[1, yy].astype(F32)
@@ -825,7 +827,8 @@
             rs_mid(4 + n, i)
         if l == 1:
             send_grads()
-        G[l].o = send_z(L[l].gwout, L[l].rzout)
+        if l == 1:
+            G[l].o = send_z(L[l].gwout, L[l].rzout)
         hook()
 
     def feedforward_backward(l, states, hook):
@@ -1115,16 +1118,17 @@
 
     def after_grads_1():
         att_grads()
-        gu_end(1)
+        ff_grads(1)
 
     def after_grads_0():
         last_grads()
         att_end(1)
+        down_third(1)
+        gu_end(1)
 
     feedforward_backward(1, none, finish_outputs)
-    states = hand_back(3, lambda: ff_push(1))
-    attention_backward(1, states, lambda: ff_grads(1))
-    states = hand_back(2, lambda: down_third(1))
+    attention_backward(1, hand_back(3), lambda: ff_push(1))
+    states = hand_back(2)
     feedforward_backward(0, states, after_grads_1)
     states = hand_back(1, lambda: ff_push(0))
     out_third(1)

time: 200 us -> 195 us (0.975)
  Pallas kernels: 199 us -> 194 us
    pallas_call x1, Pallas kernels: 197 us -> 192 us  [call(): pl.pallas_call(kernel, out_shape=[jax.ShapeDtypeStruct(shape, dtype) for...]
where the time goes in v5:
time: 195 us
  Pallas kernels  194 us (99%)
    pallas_call x1, Pallas kernels, call(): pl.pallas_call(kernel, out_shape=[jax.ShapeDtypeStruct(shape, dtype) for...  192 us

profile of v5, /device:TPU:4, one launch (start us, length us, event | category | flops | bytes accessed | tf_op | source)
XLA Modules:
  0.0 194.9 jit_solution(650385630801324102)
XLA Ops:
  0.7 191.6 %shard_map.305 = (bf16[2,1,64,256]{3,2,1,0:T(8,128)(2,1)}, bf16[2,1,64,256]{3,2,1,0:T(8,128)(2,1)}, f32[1,32]{1,0:T(1,128)}, f32[32,256]{1,0:T(8,128)}, f32[32,2...) custom-call(bf16[2,4,16,1024]{3,2,1,0:T(8,128)(2,1)} %bitcast.2, ...), custom_call_target="tpu_custom_call" | custom-call | tf_op jit(solution)/shard_map/pallas_call | solution.py:1196
  192.3 2.4 %shard_map.306 = (bf16[2,1,64,256]{3,2,1,0:T(8,128)(2,1)}, bf16[2,1,64,256]{3,2,1,0:T(8,128)(2,1)}, f32[1,32]{1,0:T(1,128)}, f32[32,256]{1,0:T(8,128)}, f32[32,2...) custom-call(bf16[2,1,64,256]{3,2,1,0:T(8,128)(2,1)} %get-tuple-eleme, ...), custom_call_target="tpu_custom_call" | custom-call | tf_op jit(solution)/shard_map/pallas_call | solution.py:1223

commit v6 on v5

--- a/solution.py
+++ b/solution.py
@@ -352,7 +352,9 @@
     def qk_second(l):
         w = L[l].wqk
         arrived(w.at[z], W[l].qk)
-        W[l].qk = to_z(w.at[z], w.at[z])
+        keys, queries = w.at[z, :, :, 128:256], w.at[z, :, :, 0:128]
+        W[l].k = to_z(keys, keys)
+        W[l].q = to_z(queries, queries)
 
     def z_first(src, w):
         sem, dst = new(), w.at[z, y, k]
@@ -564,7 +566,7 @@
     def values_of(l, zz):
         return L[l].kv[zz, :, :, :, 128:256].reshape(512, 128)
 
-    def attention_forward(l, states, hook, late):
+    def attention_forward(l, states, hook, late, sent=nothing):
         kv = L[l].kv
         direct, relayed = ([{j: new() for j in (1, 2, 3)} for _ in streams] for _ in range(2))
         from_mate = [new() for _ in streams]
@@ -575,8 +577,8 @@
             a = S[2 * l].a[i].reshape(128, 1024)
             w = L[l].wqk
             if i == 0:
-                arrived(w.at[0:3], W[l].qk)
-            qk = nn(a, w[...].reshape(1024, 256))
+                arrived(w.at[0:3, :, :, 128:256], W[l].k)
+            keys = nn(a, w[:, :, :, 128:256].reshape(1024, 128))
             w = L[l].wval
             if i == 0:
                 arrived(w.at[0:3], W[l].v)
@@ -585,19 +587,24 @@
                 values = u.astype(BF)
             else:
                 values = (0.5 * u + 0.5 * L[0].kv[z, yy, i, :, 128:256].astype(F32)).astype(BF)
-            kv[z, yy, i, :, 0:128] = qk[:, 128:256].astype(BF)
+            kv[z, yy, i, :, 0:128] = keys.astype(BF)
             kv[z, yy, i, :, 128:256] = values
             own = kv.at[z, yy, i]
             for j in (1, 3):
                 put(own, own, dev(x, plus(z, j), y, k), direct[i][j])
             put(own, own, partner, from_mate[i])
             put(own, own, dev(x, plus(z, 2), y, k), direct[i][2])
-            L[l].q2[256 * i : 256 * i + 256, :] = two_heads((qk[:, 0:128].astype(BF) * 0.125).astype(BF))
+        sent()
         for i in streams:
             near = kv.at[z, mate, i]
             arrived(near, from_mate[i])
             for j in (1, 3):
                 put(near, near, dev(x, plus(z, j), y, k), relayed[i][j])
+        w = L[l].wqk
+        arrived(w.at[0:3, :, :, 0:128], W[l].q)
+        for i in streams:
+            q = nn(S[2 * l].a[i].reshape(128, 1024), w[:, :, :, 0:128].reshape(1024, 128)).astype(BF)
+            L[l].q2[256 * i : 256 * i + 256, :] = two_heads((q * 0.125).astype(BF))
         scores = R.scores
         top = jnp.full((1, 512), MASKED, F32)
         for j in (0, 3, 1, 2):
@@ -1047,9 +1054,11 @@
     arrived(R.gz.at[0:3], gz_sem)
     R.gains[...] = jnp.concatenate([R.gz[i // 2, i % 2] for i in range(8)], axis=1)
     S[0].a[...] = (normed * gain_row(0)).astype(BF).reshape(2, 8, 16, 1024)
-    W[0].o = cross_third(L[0].wout, W[0].o)
-    W[0].d = cross_second(L[0].cwd, L[0].wdn, W[0].d)
     cot_sems = []
+
+    def after_sends_0():
+        W[0].o = cross_third(L[0].wout, W[0].o)
+        W[0].d = cross_second(L[0].cwd, L[0].wdn, W[0].d)
 
     def after_keys_0():
         ring_relay(W[0].gate)
@@ -1099,7 +1108,7 @@
             to_owners(i, rows, R.outst, R.outrv, landed.out)
 
     none = (None, None)
-    attention_forward(0, none, after_keys_0, nothing)
+    attention_forward(0, none, after_keys_0, nothing, after_sends_0)
     feedforward_forward(0, next_rows(0, in_gather_0), in_ff_0, after_ff_0)
     attention_forward(1, next_rows(1, in_gather_1), after_keys_1, after_att_1)
     feedforward_forward(1, next_rows(2, in_gather_2), nothing, take_cotangent)

time: 195 us -> 195 us (level)
  no operation moved by 1% of the time
where the time goes in v6:
time: 195 us
  Pallas kernels  194 us (99%)
    pallas_call x1, Pallas kernels, call(): pl.pallas_call(kernel, out_shape=[jax.ShapeDtypeStruct(shape, dtype) for...  192 us

profile of v6, /device:TPU:4, one launch (start us, length us, event | category | flops | bytes accessed | tf_op | source)
XLA Modules:
  0.0 194.9 jit_solution(15895722901916158415)
XLA Ops:
  0.7 191.6 %shard_map.305 = (bf16[2,1,64,256]{3,2,1,0:T(8,128)(2,1)}, bf16[2,1,64,256]{3,2,1,0:T(8,128)(2,1)}, f32[1,32]{1,0:T(1,128)}, f32[32,256]{1,0:T(8,128)}, f32[32,2...) custom-call(bf16[2,4,16,1024]{3,2,1,0:T(8,128)(2,1)} %bitcast.2, ...), custom_call_target="tpu_custom_call" | custom-call | tf_op jit(solution)/shard_map/pallas_call | solution.py:1205
  192.3 2.4 %shard_map.306 = (bf16[2,1,64,256]{3,2,1,0:T(8,128)(2,1)}, bf16[2,1,64,256]{3,2,1,0:T(8,128)(2,1)}, f32[1,32]{1,0:T(1,128)}, f32[32,256]{1,0:T(8,128)}, f32[32,2...) custom-call(bf16[2,1,64,256]{3,2,1,0:T(8,128)(2,1)} %get-tuple-eleme, ...), custom_call_target="tpu_custom_call" | custom-call | tf_op jit(solution)/shard_map/pallas_call | solution.py:1232
